TPU v7x, 32 devices: a whole 2x2x4 slice. The times are simulated.
32 devices in a mesh: outer: 4 (over z), inner: 4 (over x, core), head: 2 (over y).
Axes of the slice: x: 2, y: 2, z: 4, core: 2. Of those that a mesh axis runs over, the one named last changes fastest.
Arguments:
- query: bfloat16 [2048, 6144], P(('outer', 'inner'), 'head'), may hold values from -6 to 6
- key: bfloat16 [2048, 1024], P(('outer', 'inner', 'head')), may hold values from -6 to 6
- value: bfloat16 [2048, 1024], P(('outer', 'inner', 'head')), may hold values from -6 to 6
- output_cotangent: bfloat16 [2048, 6144], P(('outer', 'inner'), 'head'), may hold values from -6 to 6
- segment: int32 [2048], replicated, may hold values from 0 to 15, never falling along the last dimension, each value on 1 to 256 neighbouring positions
Outputs:
- attended: bfloat16 [2048, 6144], P(('outer', 'inner'), 'head')
- d_query: bfloat16 [2048, 6144], P(('outer', 'inner'), 'head')
- d_key: bfloat16 [2048, 1024], P(('outer', 'inner', 'head'))
- d_value: bfloat16 [2048, 1024], P(('outer', 'inner', 'head'))
Inputs may be any that keep to these rules, and one draw needn't show every extreme that they name: `segment`: ids never fall along the row; every document has 1 to 256 tokens, and some document has exactly 256.
All inputs are finite; a program needn't handle non-finite values.
Results may differ from a plain program's by a relative error of at most 0.03.
Values may be sent and summed in bfloat16 or wider, within the bound.
A program may use at most 64 MiB of HBM per device.

v0:
```python
import math

import jax
import jax.numpy as jnp
from jax import lax
from jax.sharding import PartitionSpec as P

QUERY_HEADS = 48
KEY_VALUE_HEADS = 8
HEAD_SIZE = 128
REACH = 2


def passed_along(x, axis, by):
    devices = lax.axis_size(axis)
    pairs = [(i, i + by) for i in range(devices) if 0 <= i + by < devices]
    return lax.ppermute(x, axis, pairs)


def block_allowed(query_seg, query_pos, segment, source, length):
    key_start = source * length
    key_seg = lax.dynamic_slice_in_dim(segment, jnp.maximum(key_start, 0), length, 0)
    key_pos = key_start + jnp.arange(length, dtype=jnp.int32)
    return (
        (query_seg[:, None] == key_seg[None, :])
        & (key_pos[None, :] <= query_pos[:, None])
        & (source >= 0)
    )


def block_scores(queries, block_key, allowed, factor):
    head_keys = block_key.reshape(block_key.shape[0], -1, HEAD_SIZE)
    scores = (
        jnp.einsum("tkgd,skd->kgts", queries, head_keys, preferred_element_type=jnp.float32)
        * factor
    )
    return jnp.where(allowed, scores, -jnp.inf)


def body(query, key, value, output_cotangent, segment):
    length = query.shape[0]
    query_group_width = QUERY_HEADS // KEY_VALUE_HEADS
    factor = 1.0 / math.sqrt(HEAD_SIZE)
    keys_here, values_here = (
        lax.all_to_all(key, "head", split_axis=1, concat_axis=0, tiled=True),
        lax.all_to_all(value, "head", split_axis=1, concat_axis=0, tiled=True),
    )
    kv_heads = keys_here.shape[1] // HEAD_SIZE
    shard_index = lax.axis_index(("outer", "inner"))
    first_row = shard_index * length
    query_seg = lax.dynamic_slice_in_dim(segment, first_row, length, 0)
    query_pos = first_row + jnp.arange(length, dtype=jnp.int32)
    queries = query.reshape(length, kv_heads, query_group_width, HEAD_SIZE)
    grads_out = output_cotangent.reshape(length, kv_heads, query_group_width, HEAD_SIZE)
    blocks = [(keys_here, values_here)]
    for offset in range(REACH):
        moved_key, moved_value = blocks[-1]
        blocks.append(passed_along((moved_key, moved_value), ("outer", "inner"), 1))
    masks = [
        block_allowed(query_seg, query_pos, segment, shard_index - offset, length)
        for offset in range(REACH + 1)
    ]
    row_max = None
    row_total = None
    for offset in range(REACH + 1):
        scores = block_scores(queries, blocks[offset][0], masks[offset], factor)
        block_max = jnp.max(scores, -1, keepdims=True)
        if offset == 0:
            row_max = block_max
            row_total = jnp.sum(jnp.exp(scores - row_max), -1, keepdims=True)
        else:
            new_max = jnp.maximum(row_max, block_max)
            row_total = row_total * jnp.exp(row_max - new_max) + jnp.sum(
                jnp.exp(scores - new_max), -1, keepdims=True
            )
            row_max = new_max
    log_total = row_max + jnp.log(row_total)
    attended_sum = jnp.zeros((length, kv_heads, query_group_width, HEAD_SIZE), jnp.float32)
    for offset in range(REACH + 1):
        block_key, block_value = blocks[offset]
        scores = block_scores(queries, block_key, masks[offset], factor)
        weights = jnp.exp(scores - log_total).astype(jnp.bfloat16)
        head_values = block_value.reshape(length, -1, HEAD_SIZE)
        attended_sum = attended_sum + jnp.einsum(
            "kgts,skd->tkgd", weights, head_values, preferred_element_type=jnp.float32
        )
    attended = attended_sum.astype(jnp.bfloat16)
    delta_row = jnp.sum(grads_out.astype(jnp.float32) * attended.astype(jnp.float32), -1)
    delta_row = jnp.transpose(delta_row, (1, 2, 0))[..., None]
    back_blocks = [(keys_here, values_here)]
    for offset in range(REACH):
        moved_key, moved_value = back_blocks[-1]
        back_blocks.append(passed_along((moved_key, moved_value), ("outer", "inner"), 1))
    grad_query = jnp.zeros((length, kv_heads, query_group_width, HEAD_SIZE), jnp.float32)
    partials = []
    for offset in range(REACH + 1):
        block_key, block_value = back_blocks[offset]
        head_keys = block_key.reshape(length, -1, HEAD_SIZE)
        head_values = block_value.reshape(length, -1, HEAD_SIZE)
        scores = block_scores(queries, block_key, masks[offset], factor)
        weights = jnp.exp(scores - log_total)
        weights_low = weights.astype(jnp.bfloat16)
        d_weights = jnp.einsum(
            "tkgd,skd->kgts", grads_out, head_values, preferred_element_type=jnp.float32
        )
        d_scores = (weights * (d_weights - delta_row)).astype(jnp.bfloat16)
        grad_query = grad_query + jnp.einsum(
            "kgts,skd->tkgd", d_scores, head_keys, preferred_element_type=jnp.float32
        )
        key_portion = (
            jnp.einsum("kgts,tkgd->skd", d_scores, queries, preferred_element_type=jnp.float32)
            * factor
        )
        value_portion = jnp.einsum(
            "kgts,tkgd->skd", weights_low, grads_out, preferred_element_type=jnp.float32
        )
        partials.append((key_portion.reshape(length, -1), value_portion.reshape(length, -1)))
    total_key, total_value = partials[REACH]
    for offset in range(REACH - 1, -1, -1):
        back_key, back_value = (
            passed_along(total_key.astype(jnp.bfloat16), ("outer", "inner"), -1).astype(
                total_key.dtype
            ),
            passed_along(total_value.astype(jnp.bfloat16), ("outer", "inner"), -1).astype(
                total_value.dtype
            ),
        )
        total_key = back_key + partials[offset][0]
        total_value = back_value + partials[offset][1]
    d_key, d_value = (
        lax.all_to_all(
            total_key.astype(jnp.bfloat16), "head", split_axis=0, concat_axis=1, tiled=True
        ),
        lax.all_to_all(
            total_value.astype(jnp.bfloat16), "head", split_axis=0, concat_axis=1, tiled=True
        ),
    )
    d_query = (grad_query * factor).astype(jnp.bfloat16).reshape(length, -1)
    return (attended.reshape(length, -1), d_query, d_key, d_value)


def solution(mesh):
    in_specs = (
        P(("outer", "inner"), "head"),
        P(("outer", "inner", "head"), None),
        P(("outer", "inner", "head"), None),
        P(("outer", "inner"), "head"),
        P(),
    )
    out_specs = (
        P(("outer", "inner"), "head"),
        P(("outer", "inner"), "head"),
        P(("outer", "inner", "head"), None),
        P(("outer", "inner", "head"), None),
    )
    return jax.shard_map(body, mesh=mesh, in_specs=in_specs, out_specs=out_specs, check_vma=False)
```

profile of v0, /device:TPU:19, one launch (start us, length us, event | category | flops | bytes accessed | tf_op | source)
XLA Modules:
  0.0 100.9 jit_solution(3959228503719294293)
XLA Ops:
  0.7 1.7 %copy.234 = bf16[8,2,8,512]{3,2,0,1:T(8,128)(2,1)} copy(bf16[8,2,8,512]{3,2,1,0:T(8,128)(2,1)} %bitcast.205) | data formatting | bytes 262144 | tf_op jit(solution)/shard_map/all_to_all | solution.py:45
  2.3 3.4 %all-to-all-start = ((bf16[64,2,512]{2,0,1:T(8,128)(2,1)}), bf16[64,2,512]{2,0,1:T(8,128)(2,1)S(1)}, u32[]{:S(2)}, u32[]{:S(2)}) async-start(bf16[64,2,512]{2,0,1:T(8,128)(2,1)} %bitcast.164), calls=%async_computation | async-start | bytes 262144 | tf_op jit(solution)/shard_map/all_to_all | solution.py:45
  9.0 4.0 %all-to-all-start.1 = ((bf16[64,2,512]{2,0,1:T(8,128)(2,1)}), bf16[64,2,512]{2,0,1:T(8,128)(2,1)}, u32[]{:S(2)}, u32[]{:S(2)}) async-start(bf16[64,2,512]{2,0,1:T(8,128)(2,1)} %bitcast.165), calls=%async_computation.1 | async-start | bytes 262144 | tf_op jit(solution)/shard_map/all_to_all | solution.py:46
  14.8 1.7 %all-to-all-done.1 = bf16[64,2,512]{2,0,1:T(8,128)(2,1)} async-done(((bf16[64,2,512]{2,0,1:T(8,128)(2,1)}), bf16[64,2,512]{2,0,1:T(8,128)(2,1)}, u32[]{:S(2)}, u32[]{:S(2)}) %all-to-all-start.1) | async-done | bytes 131104 | tf_op jit(solution)/shard_map/all_to_all | solution.py:46
  17.4 6.0 %collective-permute-start.2 = (bf16[128,512]{1,0:T(8,128)(2,1)}, bf16[128,512]{1,0:T(8,128)(2,1)}, u32[]{:S(2)}, u32[]{:S(2)}) collective-permute-start(bf16[128,512]{1,0:T(8,128)(2,1)} %bitcast.13), channel_id=1, source_target_pairs={{0,2},{2,4},{4,6},{6,8},{8,10},{10,12},{12,14},{14,16},{16,18},{18... | collective-permute-start | bytes 393224 | tf_op jit(solution)/shard_map/ppermute | solution.py:17
  23.4 1.9 %collective-permute-start = (bf16[128,512]{1,0:T(8,128)(2,1)S(1)}, bf16[128,512]{1,0:T(8,128)(2,1)}, u32[]{:S(2)}, u32[]{:S(2)}) collective-permute-start(bf16[128,512]{1,0:T(8,128)(2,1)S(1)} %bitcast.197), channel_id=1, source_target_pairs={{0,2},{2,4},{4,6},{6,8},{8,10},{10,12},{12,14},{14,16},{16,18},{18... | collective-permute-start | bytes 393224 | tf_op jit(solution)/shard_map/ppermute | solution.py:17
  28.4 5.2 %collective-permute-start.1 = (bf16[128,512]{1,0:T(8,128)(2,1)}, bf16[128,512]{1,0:T(8,128)(2,1)}, u32[]{:S(2)}, u32[]{:S(2)}) collective-permute-start(bf16[128,512]{1,0:T(8,128)(2,1)} %collective-permute-done), channel_id=1, source_target_pairs={{0,2},{2,4},{4,6},{6,8},{8,10},{10,12},{12,14},{14,16},{16,18},{18... | collective-permute-start | bytes 393224 | tf_op jit(solution)/shard_map/ppermute | solution.py:17
  33.7 2.9 %fusion.30 = (f32[4,6,128]{2,1,0:T(8,128)}, f32[4,6,128,128]{2,3,1,0:T(8,128)}) fusion(bf16[128,4,128,1]{0,2,3,1:T(8,128)(2,1)S(1)} %bitcast.185, bf16[128,4,6,128]{0,3,2,1:T(8,128)(2,1)S(1)} %bitcast.174, pred[128,128]{0,1:T(8,128)(4,1)} %get-tuple-element.26), kind=kOutput, calls=%fused_computation.56 | convolution fusion | flops 101839872 | bytes 2519040 | tf_op jit(solution)/shard_map/tkgd,skd->kgts/dot_general | solution.py:34
  36.6 1.7 %copy.141 = bf16[128,512]{0,1:T(8,128)(2,1)} copy(bf16[128,512]{1,0:T(8,128)(2,1)} %collective-permute-done.2) | data formatting | bytes 262144 | tf_op jit(solution)/shard_map/ppermute | solution.py:17
  38.3 1.9 %collective-permute-start.3 = (bf16[128,512]{1,0:T(8,128)(2,1)}, bf16[128,512]{1,0:T(8,128)(2,1)}, u32[]{:S(2)}, u32[]{:S(2)}) collective-permute-start(bf16[128,512]{1,0:T(8,128)(2,1)} %collective-permute-done.2), channel_id=1, source_target_pairs={{0,2},{2,4},{4,6},{6,8},{8,10},{10,12},{12,14},{14,16},{16,18},{18... | collective-permute-start | bytes 393224 | tf_op jit(solution)/shard_map/ppermute | solution.py:17
  45.6 1.6 %fusion.18 = f32[4,6,128,128]{2,3,1,0:T(8,128)} fusion(bf16[128,4,128,1]{0,2,3,1:T(8,128)(2,1)S(1)} %bitcast.187, f32[4,6,128,128]{2,3,1,0:T(8,128)S(1)} %copy-done, f32[4,6,128]{2,1,0:T(8,128)S(1)} %log_add_fusion), kind=kOutput, calls=%fused_computation.38 | convolution fusion | flops 101449728 | bytes 3289088 | tf_op jit(solution)/shard_map/kgts,skd->tkgd/dot_general | solution.py:84
  47.2 1.6 %fusion.22 = f32[4,6,128,128]{2,3,1,0:T(8,128)} fusion(f32[4,6,128,128]{2,3,1,0:T(8,128)S(1)} %get-tuple-element.32, f32[4,6,128]{2,1,0:T(8,128)S(1)} %log_add_fusion, bf16[128,4,128,1]{2,1,0,3:T(4,128)(2,1)S(1)} %bitcast.183), kind=kOutput, calls=%fused_computation.40 | convolution fusion | flops 101449728 | bytes 3289088 | tf_op jit(solution)/shard_map/kgts,skd->tkgd/dot_general | solution.py:84
  49.9 1.7 %copy.143 = bf16[128,512]{0,1:T(8,128)(2,1)} copy(bf16[128,512]{1,0:T(8,128)(2,1)} %collective-permute-done.3) | data formatting | bytes 262144 | tf_op jit(solution)/shard_map/ppermute | solution.py:17
  51.5 4.0 %multiply_reduce_fusion = (f32[128,4,6]{0,2,1:T(8,128)S(1)}, bf16[4,6,128,128]{2,3,1,0:T(8,128)(2,1)}) fusion(bf16[128,4,6,128]{0,3,2,1:T(8,128)(2,1)S(1)} %bitcast.169, bf16[128,4,128,1]{0,2,3,1:T(8,128)(2,1)} %bitcast.189, f32[4,6,128,128]{2,3,1,0:T(8,128)} %copy-done.2, f32[4,6,128]{2,1,0:T(8,128)S(1)} %log_add_fusion, f32[4,6,128,128]{2,3,1,0:T(8,128)} %fusion.22, ...), kind=kOutput, calls=%fused_computation.13 | convolution fusion | flops 104199168 | bytes 6447104 | tf_op jit(solution)/shard_map/kgts,skd->tkgd/dot_general | solution.py:84
  62.8 1.7 %copy.164 = bf16[128,512]{1,0:T(8,128)(2,1)} copy(bf16[128,512]{0,1:T(8,128)(2,1)} %bitcast.195) | data formatting | bytes 262144 | tf_op jit(solution)/shard_map/convert_element_type | solution.py:124
  64.5 2.4 %collective-permute-start.6 = (bf16[128,512]{1,0:T(8,128)(2,1)}, bf16[128,512]{1,0:T(8,128)(2,1)}, u32[]{:S(2)}, u32[]{:S(2)}) collective-permute-start(bf16[128,512]{1,0:T(8,128)(2,1)} %copy.164), channel_id=1, source_target_pairs={{2,0},{4,2},{6,4},{8,6},{10,8},{12,10},{14,12},{16,14},{18,16},{20... | collective-permute-start | bytes 393224 | tf_op jit(solution)/shard_map/ppermute | solution.py:17
  69.9 1.7 %copy.157 = bf16[128,512]{1,0:T(8,128)(2,1)} copy(bf16[128,512]{0,1:T(8,128)(2,1)} %bitcast.201) | data formatting | bytes 262144 | tf_op jit(solution)/shard_map/convert_element_type | solution.py:121
  71.6 1.9 %collective-permute-start.4 = (bf16[128,512]{1,0:T(8,128)(2,1)}, bf16[128,512]{1,0:T(8,128)(2,1)}, u32[]{:S(2)}, u32[]{:S(2)}) collective-permute-start(bf16[128,512]{1,0:T(8,128)(2,1)} %copy.157), channel_id=1, source_target_pairs={{2,0},{4,2},{6,4},{8,6},{10,8},{12,10},{14,12},{16,14},{18,16},{20... | collective-permute-start | bytes 393224 | tf_op jit(solution)/shard_map/ppermute | solution.py:17
  75.8 1.9 %collective-permute-start.7 = (bf16[128,512]{1,0:T(8,128)(2,1)S(1)}, bf16[128,512]{1,0:T(8,128)(2,1)S(1)}, u32[]{:S(2)}, u32[]{:S(2)}) collective-permute-start(bf16[128,512]{1,0:T(8,128)(2,1)S(1)} %add_convert_fusion.2), channel_id=1, source_target_pairs={{2,0},{4,2},{6,4},{8,6},{10,8},{12,10},{14,12},{16,14},{18,16},{20... | collective-permute-start | bytes 393224 | tf_op jit(solution)/shard_map/ppermute | solution.py:17
  80.0 2.2 %collective-permute-start.5 = (bf16[128,512]{1,0:T(8,128)(2,1)S(1)}, bf16[128,512]{1,0:T(8,128)(2,1)S(1)}, u32[]{:S(2)}, u32[]{:S(2)}) collective-permute-start(bf16[128,512]{1,0:T(8,128)(2,1)S(1)} %add_convert_fusion.4), channel_id=1, source_target_pairs={{2,0},{4,2},{6,4},{8,6},{10,8},{12,10},{14,12},{16,14},{18,16},{20... | collective-permute-start | bytes 393224 | tf_op jit(solution)/shard_map/ppermute | solution.py:17
  83.6 3.4 %all-to-all-start.3 = ((bf16[2,64,512]{2,1,0:T(8,128)(2,1)}), bf16[2,64,512]{2,1,0:T(8,128)(2,1)S(1)}, u32[]{:S(2)}, u32[]{:S(2)}) async-start(bf16[2,64,512]{2,1,0:T(8,128)(2,1)} %bitcast.63), calls=%async_computation.3 | async-start | bytes 262144 | tf_op jit(solution)/shard_map/all_to_all | solution.py:134
  87.9 3.2 %all-to-all-done.3 = bf16[2,64,512]{2,1,0:T(8,128)(2,1)S(1)} async-done(((bf16[2,64,512]{2,1,0:T(8,128)(2,1)}), bf16[2,64,512]{2,1,0:T(8,128)(2,1)S(1)}, u32[]{:S(2)}, u32[]{:S(2)}) %all-to-all-start.3) | async-done | bytes 131104 | tf_op jit(solution)/shard_map/all_to_all | solution.py:134
  91.1 3.4 %all-to-all-start.2 = ((bf16[2,64,512]{2,1,0:T(8,128)(2,1)}), bf16[2,64,512]{2,1,0:T(8,128)(2,1)S(1)}, u32[]{:S(2)}, u32[]{:S(2)}) async-start(bf16[2,64,512]{2,1,0:T(8,128)(2,1)} %bitcast.49), calls=%async_computation.2 | async-start | bytes 262144 | tf_op jit(solution)/shard_map/all_to_all | solution.py:131
  94.5 2.7 %multiply_convert_fusion = bf16[4,6,128,128]{2,3,1,0:T(8,128)(2,1)} fusion(f32[4,6,128,128]{2,3,1,0:T(8,128)} %fusion.31, f32[4,6,128,128]{2,3,1,0:T(8,128)S(1)} %fusion.32, bf16[128,4,128,1]{0,2,3,1:T(8,128)(2,1)S(1)} %bitcast.182, bf16[4,6,128,128]{2,3,1,0:T(8,128)(2,1)S(1)} %copy-done.4), kind=kOutput, calls=%fused_computation.12 | convolution fusion | flops 102236160 | bytes 4849664 | tf_op jit(solution)/shard_map/kgts,skd->tkgd/dot_general | solution.py:107
  (93 shorter events, 36.1 us)
Async XLA Ops:
  0.6 13.2 %copy-start.14 = (bf16[128,3072]{1,0:T(8,128)(2,1)S(1)}, bf16[128,3072]{1,0:T(8,128)(2,1)}, u32[]{:S(2)}) copy-start(bf16[128,3072]{1,0:T(8,128)(2,1)} %param.5) | copy-start | bytes 2359300
  0.6 13.6 %copy-start.15 = (bf16[128,3072]{1,0:T(8,128)(2,1)S(1)}, bf16[128,3072]{1,0:T(8,128)(2,1)}, u32[]{:S(2)}) copy-start(bf16[128,3072]{1,0:T(8,128)(2,1)} %param.8) | copy-start | bytes 2359300
  2.3 6.7 %all-to-all-start = ((bf16[64,2,512]{2,0,1:T(8,128)(2,1)}), bf16[64,2,512]{2,0,1:T(8,128)(2,1)S(1)}, u32[]{:S(2)}, u32[]{:S(2)}) async-start(bf16[64,2,512]{2,0,1:T(8,128)(2,1)} %bitcast.164), calls=%async_computation | async-start | bytes 262144 | tf_op jit(solution)/shard_map/all_to_all | solution.py:45
  9.0 7.4 %all-to-all-start.1 = ((bf16[64,2,512]{2,0,1:T(8,128)(2,1)}), bf16[64,2,512]{2,0,1:T(8,128)(2,1)}, u32[]{:S(2)}, u32[]{:S(2)}) async-start(bf16[64,2,512]{2,0,1:T(8,128)(2,1)} %bitcast.165), calls=%async_computation.1 | async-start | bytes 262144 | tf_op jit(solution)/shard_map/all_to_all | solution.py:46
  17.4 19.2 %collective-permute-start.2 = (bf16[128,512]{1,0:T(8,128)(2,1)}, bf16[128,512]{1,0:T(8,128)(2,1)}, u32[]{:S(2)}, u32[]{:S(2)}) collective-permute-start(bf16[128,512]{1,0:T(8,128)(2,1)} %bitcast.13), channel_id=1, source_target_pairs={{0,2},{2,4},{4,6},{6,8},{8,10},{10,12},{12,14},{14,16},{16,18},{18... | collective-permute-start | bytes 393224 | tf_op jit(solution)/shard_map/ppermute | solution.py:17
  23.4 4.0 %collective-permute-start = (bf16[128,512]{1,0:T(8,128)(2,1)S(1)}, bf16[128,512]{1,0:T(8,128)(2,1)}, u32[]{:S(2)}, u32[]{:S(2)}) collective-permute-start(bf16[128,512]{1,0:T(8,128)(2,1)S(1)} %bitcast.197), channel_id=1, source_target_pairs={{0,2},{2,4},{4,6},{6,8},{8,10},{10,12},{12,14},{14,16},{16,18},{18... | collective-permute-start | bytes 393224 | tf_op jit(solution)/shard_map/ppermute | solution.py:17
  26.5 10.1 %copy-start.16 = (f32[4,6,128]{2,1,0:T(8,128)}, f32[4,6,128]{2,1,0:T(8,128)S(1)}, u32[]{:S(2)}) copy-start(f32[4,6,128]{2,1,0:T(8,128)S(1)} %get-tuple-element.31) | copy-start | bytes 36868
  28.4 11.8 %copy-start.7 = (bf16[128,512]{0,1:T(8,128)(2,1)}, bf16[128,512]{0,1:T(8,128)(2,1)S(1)}, u32[]{:S(2)}) copy-start(bf16[128,512]{0,1:T(8,128)(2,1)S(1)} %copy.132) | copy-start | bytes 393220
  28.4 11.8 %collective-permute-start.1 = (bf16[128,512]{1,0:T(8,128)(2,1)}, bf16[128,512]{1,0:T(8,128)(2,1)}, u32[]{:S(2)}, u32[]{:S(2)}) collective-permute-start(bf16[128,512]{1,0:T(8,128)(2,1)} %collective-permute-done), channel_id=1, source_target_pairs={{0,2},{2,4},{4,6},{6,8},{8,10},{10,12},{12,14},{14,16},{16,18},{18... | collective-permute-start | bytes 393224 | tf_op jit(solution)/shard_map/ppermute | solution.py:17
  38.3 11.6 %collective-permute-start.3 = (bf16[128,512]{1,0:T(8,128)(2,1)}, bf16[128,512]{1,0:T(8,128)(2,1)}, u32[]{:S(2)}, u32[]{:S(2)}) collective-permute-start(bf16[128,512]{1,0:T(8,128)(2,1)} %collective-permute-done.2), channel_id=1, source_target_pairs={{0,2},{2,4},{4,6},{6,8},{8,10},{10,12},{12,14},{14,16},{16,18},{18... | collective-permute-start | bytes 393224 | tf_op jit(solution)/shard_map/ppermute | solution.py:17
  40.2 2.3 %copy-start.17 = (f32[4,6,128]{2,1,0:T(8,128)S(1)}, f32[4,6,128]{2,1,0:T(8,128)}, u32[]{:S(2)}) copy-start(f32[4,6,128]{2,1,0:T(8,128)} %copy-done.16) | copy-start | bytes 36868
  42.5 6.3 %copy-start.2 = (f32[4,6,128,128]{2,3,1,0:T(8,128)}, f32[4,6,128,128]{2,3,1,0:T(8,128)S(1)}, u32[]{:S(2)}) copy-start(f32[4,6,128,128]{2,3,1,0:T(8,128)S(1)} %get-tuple-element.30) | copy-start | bytes 4718596
  51.5 4.0 %copy-start.1 = (f32[4,6,128,128]{2,3,1,0:T(8,128)S(1)}, f32[4,6,128,128]{2,3,1,0:T(8,128)}, u32[]{:S(2)}) copy-start(f32[4,6,128,128]{2,3,1,0:T(8,128)} %get-tuple-element.34) | copy-start | bytes 4718596
  51.5 4.0 %copy-start.10 = (bf16[128,512]{0,1:T(8,128)(2,1)S(1)}, bf16[128,512]{0,1:T(8,128)(2,1)}, u32[]{:S(2)}) copy-start(bf16[128,512]{0,1:T(8,128)(2,1)} %copy.141) | copy-start | bytes 393220
  61.3 5.6 %copy-start.4 = (bf16[4,6,128,128]{2,3,1,0:T(8,128)(2,1)S(1)}, bf16[4,6,128,128]{2,3,1,0:T(8,128)(2,1)}, u32[]{:S(2)}) copy-start(bf16[4,6,128,128]{2,3,1,0:T(8,128)(2,1)} %fusion.1) | copy-start | bytes 2359300
  62.8 6.3 %copy-start.12 = (f32[4,128,128,1]{1,2,3,0:T(8,128)S(1)}, f32[4,128,128,1]{1,2,3,0:T(8,128)}, u32[]{:S(2)}) copy-start(f32[4,128,128,1]{1,2,3,0:T(8,128)} %fusion.16) | copy-start | bytes 786436
  64.5 10.2 %collective-permute-start.6 = (bf16[128,512]{1,0:T(8,128)(2,1)}, bf16[128,512]{1,0:T(8,128)(2,1)}, u32[]{:S(2)}, u32[]{:S(2)}) collective-permute-start(bf16[128,512]{1,0:T(8,128)(2,1)} %copy.164), channel_id=1, source_target_pairs={{2,0},{4,2},{6,4},{8,6},{10,8},{12,10},{14,12},{16,14},{18,16},{20... | collective-permute-start | bytes 393224 | tf_op jit(solution)/shard_map/ppermute | solution.py:17
  67.9 6.7 %copy-start.13 = (f32[4,128,128]{1,2,0:T(8,128)S(1)}, f32[4,128,128]{1,2,0:T(8,128)}, u32[]{:S(2)}) copy-start(f32[4,128,128]{1,2,0:T(8,128)} %fusion.11) | copy-start | bytes 786436
  71.6 7.5 %collective-permute-start.4 = (bf16[128,512]{1,0:T(8,128)(2,1)}, bf16[128,512]{1,0:T(8,128)(2,1)}, u32[]{:S(2)}, u32[]{:S(2)}) collective-permute-start(bf16[128,512]{1,0:T(8,128)(2,1)} %copy.157), channel_id=1, source_target_pairs={{2,0},{4,2},{6,4},{8,6},{10,8},{12,10},{14,12},{16,14},{18,16},{20... | collective-permute-start | bytes 393224 | tf_op jit(solution)/shard_map/ppermute | solution.py:17
  75.8 7.2 %collective-permute-start.7 = (bf16[128,512]{1,0:T(8,128)(2,1)S(1)}, bf16[128,512]{1,0:T(8,128)(2,1)S(1)}, u32[]{:S(2)}, u32[]{:S(2)}) collective-permute-start(bf16[128,512]{1,0:T(8,128)(2,1)S(1)} %add_convert_fusion.2), channel_id=1, source_target_pairs={{2,0},{4,2},{6,4},{8,6},{10,8},{12,10},{14,12},{16,14},{18,16},{20... | collective-permute-start | bytes 393224 | tf_op jit(solution)/shard_map/ppermute | solution.py:17
  80.0 7.2 %collective-permute-start.5 = (bf16[128,512]{1,0:T(8,128)(2,1)S(1)}, bf16[128,512]{1,0:T(8,128)(2,1)S(1)}, u32[]{:S(2)}, u32[]{:S(2)}) collective-permute-start(bf16[128,512]{1,0:T(8,128)(2,1)S(1)} %add_convert_fusion.4), channel_id=1, source_target_pairs={{2,0},{4,2},{6,4},{8,6},{10,8},{12,10},{14,12},{16,14},{18,16},{20... | collective-permute-start | bytes 393224 | tf_op jit(solution)/shard_map/ppermute | solution.py:17
  83.6 7.5 %all-to-all-start.3 = ((bf16[2,64,512]{2,1,0:T(8,128)(2,1)}), bf16[2,64,512]{2,1,0:T(8,128)(2,1)S(1)}, u32[]{:S(2)}, u32[]{:S(2)}) async-start(bf16[2,64,512]{2,1,0:T(8,128)(2,1)} %bitcast.63), calls=%async_computation.3 | async-start | bytes 262144 | tf_op jit(solution)/shard_map/all_to_all | solution.py:134
  91.1 9.1 %all-to-all-start.2 = ((bf16[2,64,512]{2,1,0:T(8,128)(2,1)}), bf16[2,64,512]{2,1,0:T(8,128)(2,1)S(1)}, u32[]{:S(2)}, u32[]{:S(2)}) async-start(bf16[2,64,512]{2,1,0:T(8,128)(2,1)} %bitcast.49), calls=%async_computation.2 | async-start | bytes 262144 | tf_op jit(solution)/shard_map/all_to_all | solution.py:131
  94.5 2.8 %copy-start.5 = (bf16[4,6,128,128]{2,3,1,0:T(8,128)(2,1)S(1)}, bf16[4,6,128,128]{2,3,1,0:T(8,128)(2,1)}, u32[]{:S(2)}) copy-start(bf16[4,6,128,128]{2,3,1,0:T(8,128)(2,1)} %get-tuple-element.36) | copy-start | bytes 2359300
  (9 other events, 10.8 us)
where the time goes:
time: 103 us; the launch traced here: 101 us
  starting transfers between devices  37.7 us (37%)
  matrix products  25.8 us (25%)
  local copies, waits for them, and re-layouts  21.9 us (21%)
  waiting for transfers between devices  8.04 us (8%)
  other arithmetic  6.49 us (6%)
  between operations  1.09 us (1%)
    ppermute x8, starting transfers between devices, passed_along(): return lax.ppermute(x, axis, pairs)  23.5 us
    dot_general x3, matrix products, body(): jnp.einsum('kgts,skd->tkgd', weights, head_values, preferred_element_type...  7.15 us
    ppermute x4, local copies, waits for them, and re-layouts, passed_along(): return lax.ppermute(x, axis, pairs)  5.37 us
    dot_general x3, matrix products, block_scores(): jnp.einsum('tkgd,skd->kgts', queries, head_keys, preferred_element_type=j...  5.3 us
    dot_general x3, matrix products, body(): jnp.einsum('kgts,skd->tkgd', d_scores, head_keys, preferred_element_type=...  4.61 us
    unnamed x46, local copies, waits for them, and re-layouts  4.27 us
    all_to_all x1, starting transfers between devices, body(): lax.all_to_all(value, 'head', split_axis=1, concat_axis=0, tiled=True)  4.01 us
    all_to_all x1, starting transfers between devices, body(): lax.all_to_all(total_key.astype(jnp.bfloat16), 'head', split_axis=0, conc...  3.38 us
  transfers between devices with their start and end apart: 12, of which 6 were waited for; matrix products, arithmetic and copies ran while one was open for 36% of the time, Pallas kernels for 0%

commit v1 on v0

v1 whole, which is shorter than its diff:
```python
import functools
import math

import jax
import jax.numpy as jnp
from jax import lax
from jax.experimental import pallas as pl
from jax.experimental.pallas import tpu as pltpu
from jax.sharding import PartitionSpec as P

QUERY_HEADS = 48
KEY_VALUE_HEADS = 8
HEAD_SIZE = 128
REACH = 2
GROUP = QUERY_HEADS // KEY_VALUE_HEADS
PAIR = 2
MESH = pl.DeviceIdType.MESH


def nt(a, b):
    return lax.dot_general(a, b, (((1,), (1,)), ((), ())), preferred_element_type=jnp.float32)


def tn(a, b):
    return lax.dot_general(a, b, (((0,), (0,)), ((), ())), preferred_element_type=jnp.float32)


def nn(a, b):
    return lax.dot_general(a, b, (((1,), (0,)), ((), ())), preferred_element_type=jnp.float32)


def kernel(
    inners, shards, heads,
    query_ref, key_ref, value_ref, cot_ref, seg_ref,
    att_ref, dq_ref, dk_ref, dv_ref,
    q_vm, do_vm, seg_vm, att_vm, dq_vm, kv, own, stage, got, final, bias, low,
    in_sem, seg_sem, out_sem, loc_sem,
    y_send, y_recv, f_send, f_recv, b_send, b_recv, z_send, z_recv, z_loc,
):
    D = HEAD_SIZE
    length = q_vm.shape[0]
    groups = kv.shape[3] // D
    width = groups * D
    part = length // heads
    qw = GROUP * D
    lanes = PAIR * D
    scale = 1.0 / math.sqrt(D)
    shard = lax.axis_index("outer") * inners + lax.axis_index("inner")
    me = lax.axis_index("head")

    def at_shard(target):
        return {"outer": lax.div(target, inners), "inner": lax.rem(target, inners), "head": me}

    def at_head(target):
        return {"head": target}

    def rows(p):
        return pl.ds(pl.multiple_of(p * part, part), part)

    def cols(start, size):
        return pl.ds(pl.multiple_of(start, D), size)

    def before(j):
        return lax.rem(me + heads - j, heads)

    def after(j):
        return lax.rem(me + j, heads)

    both = (key_ref, value_ref)
    outs = (dk_ref, dv_ref)

    def load(g, which):
        src, dst = ((query_ref, q_vm), (cot_ref, do_vm))[which]
        c = cols(g * qw, qw)
        return pltpu.make_async_copy(src.at[:, c], dst.at[:, c], in_sem.at[which, g])

    def save(g, which):
        src, dst = ((att_vm, att_ref), (dq_vm, dq_ref))[which]
        c = cols(g * qw, qw)
        return pltpu.make_async_copy(src.at[:, c], dst.at[:, c], out_sem.at[which, g])

    def local(g, t):
        return pltpu.make_async_copy(
            both[t].at[:, cols(me * width + g * D, D)],
            kv.at[0, t, rows(me), cols(g * D, D)],
            loc_sem.at[t, g],
        )

    def across(g, t, j):
        return pltpu.make_async_remote_copy(
            src_ref=both[t].at[:, cols(after(j) * width + g * D, D)],
            dst_ref=kv.at[0, t, rows(me), cols(g * D, D)],
            send_sem=y_send.at[j - 1, t, g],
            recv_sem=y_recv.at[j - 1, t, g],
            device_id=at_head(after(j)),
            device_id_type=MESH,
        )

    def onward(g, t, j, o):
        r = rows(before(j))
        if j == 0:
            src = both[t].at[:, cols(me * width + g * D, D)]
        else:
            src = kv.at[0, t, r, cols(g * D, D)]
        return pltpu.make_async_remote_copy(
            src_ref=src,
            dst_ref=kv.at[o, t, r, cols(g * D, D)],
            send_sem=f_send.at[o - 1, j, t, g],
            recv_sem=f_recv.at[o - 1, j, t, g],
            device_id=at_shard(shard + o),
            device_id_type=MESH,
        )

    def back(g, t, o):
        return pltpu.make_async_remote_copy(
            src_ref=stage.at[o - 1, t, :, cols(g * D, D)],
            dst_ref=got.at[o - 1, t, :, cols(g * D, D)],
            send_sem=b_send.at[o - 1, t, g],
            recv_sem=b_recv.at[o - 1, t, g],
            device_id=at_shard(shard - o),
            device_id_type=MESH,
        )

    def home(g, t, j):
        return pltpu.make_async_remote_copy(
            src_ref=final.at[t, rows(after(j)), cols(g * D, D)],
            dst_ref=outs[t].at[:, cols(me * width + g * D, D)],
            send_sem=z_send.at[j - 1, t, g],
            recv_sem=z_recv.at[j - 1, t, g],
            device_id=at_head(after(j)),
            device_id_type=MESH,
        )

    def stay(g, t):
        return pltpu.make_async_copy(
            final.at[t, rows(me), cols(g * D, D)],
            outs[t].at[:, cols(me * width + g * D, D)],
            z_loc.at[t, g],
        )

    has_next = [None] + [shard + o < shards for o in range(1, REACH + 1)]
    has_prev = [None] + [shard >= o for o in range(1, REACH + 1)]

    barrier = pltpu.get_barrier_semaphore()
    for j in range(1, heads):
        pl.semaphore_signal(barrier, inc=1, device_id=at_head(after(j)), device_id_type=MESH)
    for o in range(1, REACH + 1):
        @pl.when(has_next[o])
        def _():
            pl.semaphore_signal(barrier, inc=1, device_id=at_shard(shard + o), device_id_type=MESH)

        @pl.when(has_prev[o])
        def _():
            pl.semaphore_signal(barrier, inc=1, device_id=at_shard(shard - o), device_id_type=MESH)

    seg_copy = pltpu.make_async_copy(seg_ref, seg_vm, seg_sem)
    seg_copy.start()
    for g in range(groups):
        for t in range(2):
            local(g, t).start()
            load(g, t).start()

    for o in range(1, REACH + 1):
        @pl.when(jnp.logical_not(has_prev[o]))
        def _():
            kv[o] = jnp.zeros(kv.shape[1:], kv.dtype)

        @pl.when(jnp.logical_not(has_next[o]))
        def _():
            got[o - 1] = jnp.zeros(got.shape[1:], got.dtype)

    partners = heads - 1
    for o in range(1, REACH + 1):
        partners = partners + jnp.where(has_next[o], 1, 0) + jnp.where(has_prev[o], 1, 0)
    pl.semaphore_wait(barrier, partners)

    for g in range(groups):
        for t in range(2):
            for j in range(1, heads):
                across(g, t, j).start()
        for o in range(1, REACH + 1):
            @pl.when(has_next[o])
            def _():
                for t in range(2):
                    onward(g, t, 0, o).start()

    seg_copy.wait()

    def seg_row(o):
        row = seg_vm[pl.ds(jnp.maximum(shard - o, 0), 1), :]
        return jnp.where(shard >= o, row, -1)

    def tall(row):
        return jnp.transpose(jnp.broadcast_to(row, (length, length)))

    seg_here = seg_row(0)
    key_index = lax.broadcasted_iota(jnp.int32, (length, length), 0)
    query_index = lax.broadcasted_iota(jnp.int32, (length, length), 1)
    lower = key_index <= query_index
    merged = jnp.where(lower, tall(seg_here), tall(seg_row(2)))
    blocked = -jnp.inf
    bias_own = jnp.where(merged == seg_here, 0.0, blocked)
    bias_prev = jnp.where(tall(seg_row(1)) == seg_here, 0.0, blocked)
    one_low = jnp.where(lower, 1.0, 0.0).astype(jnp.bfloat16)
    for i in range(PAIR):
        bias[0, :, i * D:(i + 1) * D] = bias_own
        bias[1, :, i * D:(i + 1) * D] = bias_prev
        low[:, i * D:(i + 1) * D] = one_low

    for g in range(groups):
        for j in range(1, heads):
            for t in range(2):
                across(g, t, j).wait_recv()
            for o in range(1, REACH + 1):
                @pl.when(has_next[o])
                def _():
                    for t in range(2):
                        onward(g, t, j, o).start()

    wide_lower = lax.broadcasted_iota(jnp.int32, (length, lanes), 0) <= lax.rem(
        lax.broadcasted_iota(jnp.int32, (length, lanes), 1), D
    )

    def one_group(g, carry):
        for t in range(2):
            local(g, t).wait()
            load(g, t).wait()
        for o in range(1, REACH + 1):
            @pl.when(has_prev[o])
            def _():
                for j in range(heads):
                    for t in range(2):
                        onward(g, t, j, o).wait_recv()
        c = cols(g * D, D)
        order = (0, 2, 1)
        keys = jnp.concatenate([kv[o, 0, :, c] for o in order], 0)
        values = jnp.concatenate([kv[o, 1, :, c] for o in order], 0)
        dk_sum = None
        for u in range(GROUP // PAIR):
            first = g * qw + u * lanes
            spans = [cols(first + i * D, D) for i in range(PAIR)]
            q = jnp.concatenate([q_vm[:, s] for s in spans], 0)
            do = jnp.concatenate([do_vm[:, s] for s in spans], 0)
            scores = nt(keys, q)
            d_w = nt(values, do)
            s_own = jnp.where(wide_lower, scores[:length], scores[length:2 * length]) + bias[0]
            s_prev = scores[2 * length:] + bias[1]
            top = jnp.maximum(
                jnp.max(s_own, 0, keepdims=True), jnp.max(s_prev, 0, keepdims=True)
            )
            unit = scale * math.log2(math.e)
            e_own = jnp.exp2((s_own - top) * unit)
            e_prev = jnp.exp2((s_prev - top) * unit)
            inv = 1.0 / (
                jnp.sum(e_own, 0, keepdims=True) + jnp.sum(e_prev, 0, keepdims=True)
            )
            w_own = e_own * inv
            w_prev = e_prev * inv
            r_own = w_own.astype(jnp.bfloat16)
            r_prev = w_prev.astype(jnp.bfloat16)
            d_own = jnp.where(wide_lower, d_w[:length], d_w[length:2 * length])
            d_prev = d_w[2 * length:]
            delta = jnp.sum(r_own.astype(jnp.float32) * d_own, 0, keepdims=True) + jnp.sum(
                r_prev.astype(jnp.float32) * d_prev, 0, keepdims=True
            )
            g_own = (w_own * (d_own - delta)).astype(jnp.bfloat16)
            g_prev = (w_prev * (d_prev - delta)).astype(jnp.bfloat16)
            keep = low[...]
            r_low = r_own * keep
            g_low = g_own * keep
            weights = jnp.concatenate([r_low, r_own - r_low, r_prev], 0)
            d_scores = jnp.concatenate([g_low, g_own - g_low, g_prev], 0)
            att = jnp.transpose(tn(values, weights))
            dq = jnp.transpose(tn(keys, d_scores) * scale)
            for i, s in enumerate(spans):
                att_vm[:, s] = att[i * length:(i + 1) * length].astype(jnp.bfloat16)
                dq_vm[:, s] = dq[i * length:(i + 1) * length].astype(jnp.bfloat16)
            dk_part = nn(d_scores, q)
            dv_part = nn(weights, do)
            dk_sum = dk_part if dk_sum is None else dk_sum + dk_part
            dv_sum = dv_part if u == 0 else dv_sum + dv_part
        for t, total in enumerate((dk_sum * scale, dv_sum)):
            for at, o in enumerate(order):
                block = total[at * length:(at + 1) * length]
                if o == 0:
                    own[t, :, c] = block
                else:
                    stage[o - 1, t, :, c] = block.astype(jnp.bfloat16)
        for o in range(REACH, 0, -1):
            @pl.when(has_prev[o])
            def _():
                for t in range(2):
                    back(g, t, o).start()
        for t in range(2):
            save(g, t).start()
        return carry

    lax.fori_loop(0, groups, one_group, 0)

    for g in range(groups):
        c = cols(g * D, D)
        for o in range(1, REACH + 1):
            @pl.when(has_next[o])
            def _():
                for t in range(2):
                    back(g, t, o).wait_recv()
        for t in range(2):
            total = own[t, :, c]
            for o in range(1, REACH + 1):
                total = total + got[o - 1, t, :, c].astype(jnp.float32)
            final[t, :, c] = total.astype(jnp.bfloat16)
            for j in range(1, heads):
                home(g, t, j).start()
            stay(g, t).start()

    for g in range(groups):
        for t in range(2):
            save(g, t).wait()
            stay(g, t).wait()
            for j in range(1, heads):
                across(g, t, j).wait_send()
                home(g, t, j).wait()
        for o in range(1, REACH + 1):
            @pl.when(has_next[o])
            def _():
                for j in range(heads):
                    for t in range(2):
                        onward(g, t, j, o).wait_send()

            @pl.when(has_prev[o])
            def _():
                for t in range(2):
                    back(g, t, o).wait_send()


def body(mesh, query, key, value, output_cotangent, segment):
    length, wide = query.shape
    part, kv_wide = key.shape
    heads = mesh.shape["head"]
    inners = mesh.shape["inner"]
    shards = mesh.shape["outer"] * inners
    groups = kv_wide // heads // HEAD_SIZE
    width = groups * HEAD_SIZE
    bf, f32 = jnp.bfloat16, jnp.float32
    dma = pltpu.SemaphoreType.DMA
    peers = max(heads - 1, 1)
    lanes = PAIR * HEAD_SIZE
    return pl.pallas_call(
        functools.partial(kernel, inners, shards, heads),
        out_shape=(
            jax.ShapeDtypeStruct((length, wide), bf),
            jax.ShapeDtypeStruct((length, wide), bf),
            jax.ShapeDtypeStruct((part, kv_wide), bf),
            jax.ShapeDtypeStruct((part, kv_wide), bf),
        ),
        in_specs=[pl.BlockSpec(memory_space=pl.ANY)] * 5,
        out_specs=[pl.BlockSpec(memory_space=pl.ANY)] * 4,
        scratch_shapes=[
            pltpu.VMEM((length, wide), bf),
            pltpu.VMEM((length, wide), bf),
            pltpu.VMEM((shards, length), jnp.int32),
            pltpu.VMEM((length, wide), bf),
            pltpu.VMEM((length, wide), bf),
            pltpu.VMEM((REACH + 1, 2, length, width), bf),
            pltpu.VMEM((2, length, width), f32),
            pltpu.VMEM((REACH, 2, length, width), bf),
            pltpu.VMEM((REACH, 2, length, width), bf),
            pltpu.VMEM((2, length, width), bf),
            pltpu.VMEM((2, length, lanes), f32),
            pltpu.VMEM((length, lanes), bf),
            dma((2, groups)),
            dma(()),
            dma((2, groups)),
            dma((2, groups)),
            dma((peers, 2, groups)),
            dma((peers, 2, groups)),
            dma((REACH, heads, 2, groups)),
            dma((REACH, heads, 2, groups)),
            dma((REACH, 2, groups)),
            dma((REACH, 2, groups)),
            dma((peers, 2, groups)),
            dma((peers, 2, groups)),
            dma((2, groups)),
        ],
        compiler_params=pltpu.CompilerParams(
            collective_id=0, has_side_effects=True, vmem_limit_bytes=60 * 2**20
        ),
        name="packed_attention",
    )(query, key, value, output_cotangent, segment.reshape(shards, length))


def solution(mesh):
    in_specs = (
        P(("outer", "inner"), "head"),
        P(("outer", "inner", "head"), None),
        P(("outer", "inner", "head"), None),
        P(("outer", "inner"), "head"),
        P(),
    )
    out_specs = (
        P(("outer", "inner"), "head"),
        P(("outer", "inner"), "head"),
        P(("outer", "inner", "head"), None),
        P(("outer", "inner", "head"), None),
    )
    return jax.shard_map(
        functools.partial(body, mesh),
        mesh=mesh, in_specs=in_specs, out_specs=out_specs, check_vma=False,
    )
```

time: 103 us -> 33.6 us (0.33); the launches traced: 101 us -> 33.1 us
  starting transfers between devices: 37.7 us -> 0 us
  Pallas kernels: 0 us -> 27.7 us
  matrix products: 25.8 us -> 0 us
  local copies, waits for them, and re-layouts: 21.9 us -> 4.77 us
  waiting for transfers between devices: 8.04 us -> 0 us
  other arithmetic: 6.49 us -> 0 us
    pallas_call x0 -> x1, Pallas kernels: none -> 27.7 us  [body(): pl.pallas_call(functools.partial(kernel, inners, shards, heads), out_shap...]
    dot_general x18 -> x0, matrix products: 25.8 us -> none  [the longest x3 7.15 us: body(): jnp.einsum('kgts,skd->tkgd', weights, head_values, preferred_element_type...]
    ppermute x8 -> x0, starting transfers between devices: 23.5 us -> none  [passed_along(): return lax.ppermute(x, axis, pairs)]
    all_to_all x4 -> x0, starting transfers between devices: 14.1 us -> none  [the longest x1 4.01 us: body(): lax.all_to_all(value, 'head', split_axis=1, concat_axis=0, tiled=True)]
    all_to_all x4 -> x0, waiting for transfers between devices: 5.71 us -> none  [the longest x1 3.25 us: body(): lax.all_to_all(total_value.astype(jnp.bfloat16), 'head', split_axis=0, co...]
    ppermute x4 -> x0, local copies, waits for them, and re-layouts: 5.37 us -> none  [passed_along(): return lax.ppermute(x, axis, pairs)]
    all_to_all x4 -> x0, local copies, waits for them, and re-layouts: 4.58 us -> none  [the longest x1 1.68 us: body(): lax.all_to_all(key, 'head', split_axis=1, concat_axis=0, tiled=True)]
    reshape x7 -> x0, local copies, waits for them, and re-layouts: 4.28 us -> none  [the longest x2 1.96 us: body(): value_portion.reshape(length, -1)]
  transfers between devices with their start and end apart: 12 -> 0, of which waited for: 6 -> 0; matrix products, arithmetic and copies ran while one was open for 36% -> 0% of each run, Pallas kernels for 0% -> 0%
where the time goes in v1:
time: 33.6 us; the launch traced here: 33.1 us
  Pallas kernels  27.7 us (82%)
  local copies, waits for them, and re-layouts  4.77 us (14%)
  between operations  0.65 us (2%)
    pallas_call x1, Pallas kernels, body(): pl.pallas_call(functools.partial(kernel, inners, shards, heads), out_shap...  27.7 us
    unnamed x10, local copies, waits for them, and re-layouts  4.77 us

profile of v1, /device:TPU:19, one launch (start us, length us, event | category | flops | bytes accessed | tf_op | source)
XLA Modules:
  0.0 33.1 jit_solution(14630348617985319441)
XLA Ops:
  0.6 27.7 %packed_attention.1 = (bf16[128,3072]{1,0:T(8,128)(2,1)}, bf16[128,3072]{1,0:T(8,128)(2,1)}, bf16[64,1024]{1,0:T(8,128)(2,1)}, bf16[64,1024]{1,0:T(8,128)(2,1)}) custom-call(bf16[128,3072]{1,0:T(8,128)(2,1)} %query_ref.1, bf16[64,1024]{1,0:T(8,128)(2,1)} %key_ref.1, bf16[64,1024]{1,0:T(8,128)(2,1)} %value_ref.1, bf16[128,3072]{1,0:T(8,128)(2,1)} %cot_ref.1, ...), custom_call_target="tpu_custom_call" | custom-call | tf_op jit(solution)/shard_map/packed_attention/pallas_call | solution.py:348
  28.3 0.0 copy-start
  28.3 2.1 %copy.13 = bf16[128,3072]{1,0:T(8,128)(2,1)} copy(bf16[128,3072]{1,0:T(8,128)(2,1)} %get-tuple-element.8) | data formatting | bytes 1572864
  30.5 0.0 copy-done
  30.5 0.0 copy-start.2
  30.5 0.9 %copy.14 = bf16[128,3072]{1,0:T(8,128)(2,1)} copy(bf16[128,3072]{1,0:T(8,128)(2,1)S(1)} %copy-done) | data formatting | bytes 1572864
  31.3 0.1 copy-done.2
  31.5 0.0 copy-start.1
  31.5 0.7 %copy.15 = bf16[64,1024]{1,0:T(8,128)(2,1)} copy(bf16[64,1024]{1,0:T(8,128)(2,1)S(1)} %copy-done.2) | data formatting | bytes 262144
  32.1 0.3 copy-done.1
  32.4 0.7 %copy.16 = bf16[64,1024]{1,0:T(8,128)(2,1)} copy(bf16[64,1024]{1,0:T(8,128)(2,1)S(1)} %copy-done.1) | data formatting | bytes 262144
Async XLA Ops:
  28.3 2.1 %copy-start = (bf16[128,3072]{1,0:T(8,128)(2,1)S(1)}, bf16[128,3072]{1,0:T(8,128)(2,1)}, u32[]{:S(2)}) copy-start(bf16[128,3072]{1,0:T(8,128)(2,1)} %get-tuple-element.9) | copy-start | bytes 2359300
  30.5 1.0 %copy-start.2 = (bf16[64,1024]{1,0:T(8,128)(2,1)S(1)}, bf16[64,1024]{1,0:T(8,128)(2,1)}, u32[]{:S(2)}) copy-start(bf16[64,1024]{1,0:T(8,128)(2,1)} %get-tuple-element.10) | copy-start | bytes 393220
  31.5 1.0 %copy-start.1 = (bf16[64,1024]{1,0:T(8,128)(2,1)S(1)}, bf16[64,1024]{1,0:T(8,128)(2,1)}, u32[]{:S(2)}) copy-start(bf16[64,1024]{1,0:T(8,128)(2,1)} %get-tuple-element.11) | copy-start | bytes 393220

commit v2 on v1

--- a/solution.py
+++ b/solution.py
@@ -33,9 +33,9 @@
     inners, shards, heads,
     query_ref, key_ref, value_ref, cot_ref, seg_ref,
     att_ref, dq_ref, dk_ref, dv_ref,
-    q_vm, do_vm, seg_vm, att_vm, dq_vm, kv, own, stage, got, final, bias, low,
-    in_sem, seg_sem, out_sem, loc_sem,
-    y_send, y_recv, f_send, f_recv, b_send, b_recv, z_send, z_recv, z_loc,
+    q_vm, do_vm, seg_vm, kv, own, hold, mid, stage, got, final, bias, low,
+    in_sem, seg_sem, loc_sem,
+    y_send, y_recv, f_send, f_recv, r_send, m_recv, b_send, b_recv, z_send, z_recv, z_loc,
 ):
     D = HEAD_SIZE
     length = q_vm.shape[0]
@@ -74,11 +74,6 @@
         c = cols(g * qw, qw)
         return pltpu.make_async_copy(src.at[:, c], dst.at[:, c], in_sem.at[which, g])
 
-    def save(g, which):
-        src, dst = ((att_vm, att_ref), (dq_vm, dq_ref))[which]
-        c = cols(g * qw, qw)
-        return pltpu.make_async_copy(src.at[:, c], dst.at[:, c], out_sem.at[which, g])
-
     def local(g, t):
         return pltpu.make_async_copy(
             both[t].at[:, cols(me * width + g * D, D)],
@@ -111,6 +106,27 @@
             device_id_type=MESH,
         )
 
+    def relay(g, t, j):
+        r = rows(before(j))
+        return pltpu.make_async_remote_copy(
+            src_ref=kv.at[1, t, r, cols(g * D, D)],
+            dst_ref=kv.at[2, t, r, cols(g * D, D)],
+            send_sem=r_send.at[j, t, g],
+            recv_sem=f_recv.at[1, j, t, g],
+            device_id=at_shard(shard + 1),
+            device_id_type=MESH,
+        )
+
+    def back_near(g, t):
+        return pltpu.make_async_remote_copy(
+            src_ref=stage.at[1, t, :, cols(g * D, D)],
+            dst_ref=mid.at[t, :, cols(g * D, D)],
+            send_sem=b_send.at[1, t, g],
+            recv_sem=m_recv.at[t, g],
+            device_id=at_shard(shard - 1),
+            device_id_type=MESH,
+        )
+
     def back(g, t, o):
         return pltpu.make_async_remote_copy(
             src_ref=stage.at[o - 1, t, :, cols(g * D, D)],
@@ -141,15 +157,21 @@
     has_next = [None] + [shard + o < shards for o in range(1, REACH + 1)]
     has_prev = [None] + [shard >= o for o in range(1, REACH + 1)]
 
+    even = lax.rem(shard, 2) == 0
+    odd = jnp.logical_not(even)
+    deals_next = [None, has_next[1], jnp.logical_and(even, has_next[2])]
+    deals_prev = [None, has_prev[1], jnp.logical_and(even, has_prev[2])]
+    relays = deals_prev[2]
+
     barrier = pltpu.get_barrier_semaphore()
     for j in range(1, heads):
         pl.semaphore_signal(barrier, inc=1, device_id=at_head(after(j)), device_id_type=MESH)
     for o in range(1, REACH + 1):
-        @pl.when(has_next[o])
+        @pl.when(deals_next[o])
         def _():
             pl.semaphore_signal(barrier, inc=1, device_id=at_shard(shard + o), device_id_type=MESH)
 
-        @pl.when(has_prev[o])
+        @pl.when(deals_prev[o])
         def _():
             pl.semaphore_signal(barrier, inc=1, device_id=at_shard(shard - o), device_id_type=MESH)
 
@@ -165,21 +187,21 @@
         def _():
             kv[o] = jnp.zeros(kv.shape[1:], kv.dtype)
 
-        @pl.when(jnp.logical_not(has_next[o]))
+        @pl.when(jnp.logical_not(deals_next[o]))
         def _():
             got[o - 1] = jnp.zeros(got.shape[1:], got.dtype)
 
     partners = heads - 1
     for o in range(1, REACH + 1):
-        partners = partners + jnp.where(has_next[o], 1, 0) + jnp.where(has_prev[o], 1, 0)
+        partners = partners + jnp.where(deals_next[o], 1, 0) + jnp.where(deals_prev[o], 1, 0)
     pl.semaphore_wait(barrier, partners)
 
     for g in range(groups):
         for t in range(2):
             for j in range(1, heads):
                 across(g, t, j).start()
-        for o in range(1, REACH + 1):
-            @pl.when(has_next[o])
+        for o in range(REACH, 0, -1):
+            @pl.when(deals_next[o])
             def _():
                 for t in range(2):
                     onward(g, t, 0, o).start()
@@ -211,8 +233,8 @@
         for j in range(1, heads):
             for t in range(2):
                 across(g, t, j).wait_recv()
-            for o in range(1, REACH + 1):
-                @pl.when(has_next[o])
+            for o in range(REACH, 0, -1):
+                @pl.when(deals_next[o])
                 def _():
                     for t in range(2):
                         onward(g, t, j, o).start()
@@ -220,6 +242,15 @@
     wide_lower = lax.broadcasted_iota(jnp.int32, (length, lanes), 0) <= lax.rem(
         lax.broadcasted_iota(jnp.int32, (length, lanes), 1), D
     )
+
+    def merge(g):
+        c = cols(g * D, D)
+        for t in range(2):
+            back_near(g, t).wait_recv()
+            stage[0, t, :, c] = (hold[t, :, c] + mid[t, :, c].astype(jnp.float32)).astype(
+                jnp.bfloat16
+            )
+            back(g, t, 1).start()
 
     def one_group(g, carry):
         for t in range(2):
@@ -231,6 +262,13 @@
                 for j in range(heads):
                     for t in range(2):
                         onward(g, t, j, o).wait_recv()
+
+            if o == 1:
+                @pl.when(relays)
+                def _():
+                    for j in range(heads):
+                        for t in range(2):
+                            relay(g, t, j).start()
         c = cols(g * D, D)
         order = (0, 2, 1)
         keys = jnp.concatenate([kv[o, 0, :, c] for o in order], 0)
@@ -273,8 +311,8 @@
             att = jnp.transpose(tn(values, weights))
             dq = jnp.transpose(tn(keys, d_scores) * scale)
             for i, s in enumerate(spans):
-                att_vm[:, s] = att[i * length:(i + 1) * length].astype(jnp.bfloat16)
-                dq_vm[:, s] = dq[i * length:(i + 1) * length].astype(jnp.bfloat16)
+                att_ref[:, s] = att[i * length:(i + 1) * length].astype(jnp.bfloat16)
+                dq_ref[:, s] = dq[i * length:(i + 1) * length].astype(jnp.bfloat16)
             dk_part = nn(d_scores, q)
             dv_part = nn(weights, do)
             dk_sum = dk_part if dk_sum is None else dk_sum + dk_part
@@ -284,23 +322,42 @@
                 block = total[at * length:(at + 1) * length]
                 if o == 0:
                     own[t, :, c] = block
+                elif o == 1:
+                    hold[t, :, c] = block
                 else:
-                    stage[o - 1, t, :, c] = block.astype(jnp.bfloat16)
-        for o in range(REACH, 0, -1):
-            @pl.when(has_prev[o])
-            def _():
-                for t in range(2):
-                    back(g, t, o).start()
-        for t in range(2):
-            save(g, t).start()
+                    stage[1, t, :, c] = block.astype(jnp.bfloat16)
+
+        @pl.when(relays)
+        def _():
+            for t in range(2):
+                back(g, t, 2).start()
+
+            @pl.when(g >= 1)
+            def _():
+                merge(g - 1)
+
+        @pl.when(jnp.logical_and(odd, has_prev[2]))
+        def _():
+            for t in range(2):
+                back_near(g, t).start()
+
+        @pl.when(odd)
+        def _():
+            for t in range(2):
+                stage[0, t, :, c] = hold[t, :, c].astype(jnp.bfloat16)
+                back(g, t, 1).start()
         return carry
 
     lax.fori_loop(0, groups, one_group, 0)
+
+    @pl.when(relays)
+    def _():
+        merge(groups - 1)
 
     for g in range(groups):
         c = cols(g * D, D)
         for o in range(1, REACH + 1):
-            @pl.when(has_next[o])
+            @pl.when(deals_next[o])
             def _():
                 for t in range(2):
                     back(g, t, o).wait_recv()
@@ -315,13 +372,12 @@
 
     for g in range(groups):
         for t in range(2):
-            save(g, t).wait()
             stay(g, t).wait()
             for j in range(1, heads):
                 across(g, t, j).wait_send()
                 home(g, t, j).wait()
         for o in range(1, REACH + 1):
-            @pl.when(has_next[o])
+            @pl.when(deals_next[o])
             def _():
                 for j in range(heads):
                     for t in range(2):
@@ -331,6 +387,28 @@
             def _():
                 for t in range(2):
                     back(g, t, o).wait_send()
+
+        @pl.when(relays)
+        def _():
+            for j in range(heads):
+                for t in range(2):
+                    relay(g, t, j).wait_send()
+
+
+def write_out(*refs):
+    count = len(refs) // 2
+    sems = refs[-1]
+    copies = []
+    for i in range(count):
+        src, dst = refs[i], refs[count + i]
+        half = src.shape[0] // 2
+        for k in range(2):
+            r = pl.ds(k * half, half)
+            copies.append(pltpu.make_async_copy(src.at[r], dst.at[r], sems.at[i, k]))
+    for copy in copies:
+        copy.start()
+    for copy in copies:
+        copy.wait()
 
 
 def body(mesh, query, key, value, output_cotangent, segment):
@@ -345,24 +423,20 @@
     dma = pltpu.SemaphoreType.DMA
     peers = max(heads - 1, 1)
     lanes = PAIR * HEAD_SIZE
-    return pl.pallas_call(
+    shapes = ((length, wide), (length, wide), (part, kv_wide), (part, kv_wide))
+    results = pl.pallas_call(
         functools.partial(kernel, inners, shards, heads),
-        out_shape=(
-            jax.ShapeDtypeStruct((length, wide), bf),
-            jax.ShapeDtypeStruct((length, wide), bf),
-            jax.ShapeDtypeStruct((part, kv_wide), bf),
-            jax.ShapeDtypeStruct((part, kv_wide), bf),
-        ),
-        in_specs=[pl.BlockSpec(memory_space=pl.ANY)] * 5,
-        out_specs=[pl.BlockSpec(memory_space=pl.ANY)] * 4,
+        out_shape=tuple(pltpu.VMEM(shape, bf) for shape in shapes),
+        in_specs=[pl.BlockSpec(memory_space=pltpu.HBM)] * 5,
+        out_specs=[pl.BlockSpec(memory_space=pltpu.VMEM)] * 4,
         scratch_shapes=[
             pltpu.VMEM((length, wide), bf),
             pltpu.VMEM((length, wide), bf),
             pltpu.VMEM((shards, length), jnp.int32),
-            pltpu.VMEM((length, wide), bf),
-            pltpu.VMEM((length, wide), bf),
             pltpu.VMEM((REACH + 1, 2, length, width), bf),
             pltpu.VMEM((2, length, width), f32),
+            pltpu.VMEM((2, length, width), f32),
+            pltpu.VMEM((2, length, width), bf),
             pltpu.VMEM((REACH, 2, length, width), bf),
             pltpu.VMEM((REACH, 2, length, width), bf),
             pltpu.VMEM((2, length, width), bf),
@@ -371,11 +445,12 @@
             dma((2, groups)),
             dma(()),
             dma((2, groups)),
-            dma((2, groups)),
             dma((peers, 2, groups)),
             dma((peers, 2, groups)),
             dma((REACH, heads, 2, groups)),
             dma((REACH, heads, 2, groups)),
+            dma((heads, 2, groups)),
+            dma((2, groups)),
             dma((REACH, 2, groups)),
             dma((REACH, 2, groups)),
             dma((peers, 2, groups)),
@@ -383,10 +458,18 @@
             dma((2, groups)),
         ],
         compiler_params=pltpu.CompilerParams(
-            collective_id=0, has_side_effects=True, vmem_limit_bytes=60 * 2**20
+            collective_id=0, has_side_effects=True, vmem_limit_bytes=61 * 2**20
         ),
         name="packed_attention",
     )(query, key, value, output_cotangent, segment.reshape(shards, length))
+    return pl.pallas_call(
+        write_out,
+        out_shape=tuple(jax.ShapeDtypeStruct(shape, bf) for shape in shapes),
+        in_specs=[pl.BlockSpec(memory_space=pltpu.VMEM)] * 4,
+        out_specs=[pl.BlockSpec(memory_space=pltpu.HBM)] * 4,
+        scratch_shapes=[dma((len(shapes), 2))],
+        name="write_out",
+    )(*results)
 
 
 def solution(mesh):

time: 33.6 us -> 32.3 us (0.961)
  local copies, waits for them, and re-layouts: 4.77 us -> 3.08 us
  Pallas kernels: 27.7 us -> 28.4 us
    pallas_call x0 -> x1, Pallas kernels: none -> 2.7 us  [body(): pl.pallas_call(write_out, out_shape=tuple((jax.ShapeDtypeStruct(shape, bf...]
    pallas_call x1, Pallas kernels: 27.7 us -> 25.7 us  [body(): pl.pallas_call(functools.partial(kernel, inners, shards, heads), out_shap...]
    unnamed x10 -> x8, local copies, waits for them, and re-layouts: 4.77 us -> 3.08 us
where the time goes in v2:
time: 32.3 us; the launch traced here: 32.1 us
  Pallas kernels  28.4 us (88%)
  local copies, waits for them, and re-layouts  3.08 us (10%)
  between operations  0.65 us (2%)
    pallas_call x1, Pallas kernels, body(): pl.pallas_call(functools.partial(kernel, inners, shards, heads), out_shap...  25.7 us
    unnamed x8, local copies, waits for them, and re-layouts  3.08 us
    pallas_call x1, Pallas kernels, body(): pl.pallas_call(write_out, out_shape=tuple((jax.ShapeDtypeStruct(shape, bf...  2.7 us

profile of v2, /device:TPU:19, one launch (start us, length us, event | category | flops | bytes accessed | tf_op | source)
XLA Modules:
  0.0 32.1 jit_solution(14526158026556228928)
XLA Ops:
  0.6 25.7 %packed_attention.1 = (bf16[128,3072]{1,0:T(8,128)(2,1)S(1)}, bf16[128,3072]{1,0:T(8,128)(2,1)S(1)}, bf16[64,1024]{1,0:T(8,128)(2,1)S(1)}, bf16[64,1024]{1,0:T(8,128)(2,1)S(1)}) custom-call(bf16[128,3072]{1,0:T(8,128)(2,1)} %query_ref.1, bf16[64,1024]{1,0:T(8,128)(2,1)} %key_ref.1, bf16[64,1024]{1,0:T(8,128)(2,1)} %value_ref.1, bf16[128,3072]{1,0:T(8,128)(2,1)} %cot_ref.1, ...), custom_call_target="tpu_custom_call" | custom-call | tf_op jit(solution)/shard_map/packed_attention/pallas_call | solution.py:427
  26.3 0.0 copy-start
  26.4 0.9 %copy-done = bf16[128,3072]{1,0:T(8,128)(2,1)} copy-done((bf16[128,3072]{1,0:T(8,128)(2,1)}, bf16[128,3072]{1,0:T(8,128)(2,1)S(1)}, u32[]{:S(2)}) %copy-start) | copy-done | bytes 786456
  27.2 0.0 copy-start.1
  27.2 0.9 %copy-done.1 = bf16[128,3072]{1,0:T(8,128)(2,1)} copy-done((bf16[128,3072]{1,0:T(8,128)(2,1)}, bf16[128,3072]{1,0:T(8,128)(2,1)S(1)}, u32[]{:S(2)}) %copy-start.1) | copy-done | bytes 786456
  28.1 0.0 copy-start.2
  28.1 0.7 %copy-done.2 = bf16[64,1024]{1,0:T(8,128)(2,1)} copy-done((bf16[64,1024]{1,0:T(8,128)(2,1)}, bf16[64,1024]{1,0:T(8,128)(2,1)S(1)}, u32[]{:S(2)}) %copy-start.2) | copy-done | bytes 131096
  28.8 0.0 copy-start.3
  28.8 0.6 %copy-done.3 = bf16[64,1024]{1,0:T(8,128)(2,1)} copy-done((bf16[64,1024]{1,0:T(8,128)(2,1)}, bf16[64,1024]{1,0:T(8,128)(2,1)S(1)}, u32[]{:S(2)}) %copy-start.3) | copy-done | bytes 131096
  29.4 2.7 %write_out.1 = (bf16[128,3072]{1,0:T(8,128)(2,1)}, bf16[128,3072]{1,0:T(8,128)(2,1)}, bf16[64,1024]{1,0:T(8,128)(2,1)}, bf16[64,1024]{1,0:T(8,128)(2,1)}) custom-call(bf16[128,3072]{1,0:T(8,128)(2,1)} %copy-done, bf16[128,3072]{1,0:T(8,128)(2,1)} %copy-done.1, bf16[64,1024]{1,0:T(8,128)(2,1)} %copy-done.2, bf16[64,1024]{1,0:T(8,128)(2,1)} %copy-done.3), custom_call_target="tpu_custom_call" | custom-call | tf_op jit(solution)/shard_map/write_out/pallas_call | solution.py:465
Async XLA Ops:
  26.3 0.9 %copy-start = (bf16[128,3072]{1,0:T(8,128)(2,1)}, bf16[128,3072]{1,0:T(8,128)(2,1)S(1)}, u32[]{:S(2)}) copy-start(bf16[128,3072]{1,0:T(8,128)(2,1)S(1)} %get-tuple-element.8.refs_0_) | copy-start | bytes 2359300
  27.2 0.9 %copy-start.1 = (bf16[128,3072]{1,0:T(8,128)(2,1)}, bf16[128,3072]{1,0:T(8,128)(2,1)S(1)}, u32[]{:S(2)}) copy-start(bf16[128,3072]{1,0:T(8,128)(2,1)S(1)} %get-tuple-element.9.refs_1_) | copy-start | bytes 2359300
  28.1 0.7 %copy-start.2 = (bf16[64,1024]{1,0:T(8,128)(2,1)}, bf16[64,1024]{1,0:T(8,128)(2,1)S(1)}, u32[]{:S(2)}) copy-start(bf16[64,1024]{1,0:T(8,128)(2,1)S(1)} %get-tuple-element.10.refs_2_) | copy-start | bytes 393220
  28.8 0.6 %copy-start.3 = (bf16[64,1024]{1,0:T(8,128)(2,1)}, bf16[64,1024]{1,0:T(8,128)(2,1)S(1)}, u32[]{:S(2)}) copy-start(bf16[64,1024]{1,0:T(8,128)(2,1)S(1)} %get-tuple-element.11.refs_3_) | copy-start | bytes 393220

commit v3 on v2

--- a/solution.py
+++ b/solution.py
@@ -33,7 +33,7 @@
     inners, shards, heads,
     query_ref, key_ref, value_ref, cot_ref, seg_ref,
     att_ref, dq_ref, dk_ref, dv_ref,
-    q_vm, do_vm, seg_vm, kv, own, hold, mid, stage, got, final, bias, low,
+    q_vm, do_vm, seg_vm, kv, own, hold, mid, stage, got, final, bias, low, w_vm, ds_vm,
     in_sem, seg_sem, loc_sem,
     y_send, y_recv, f_send, f_recv, r_send, m_recv, b_send, b_recv, z_send, z_recv, z_loc,
 ):
@@ -243,6 +243,8 @@
         lax.broadcasted_iota(jnp.int32, (length, lanes), 1), D
     )
 
+    order = (0, 2, 1)
+
     def merge(g):
         c = cols(g * D, D)
         for t in range(2):
@@ -270,23 +272,22 @@
                         for t in range(2):
                             relay(g, t, j).start()
         c = cols(g * D, D)
-        order = (0, 2, 1)
         keys = jnp.concatenate([kv[o, 0, :, c] for o in order], 0)
         values = jnp.concatenate([kv[o, 1, :, c] for o in order], 0)
-        dk_sum = None
+        heads_q = []
+        first_q = g * qw
         for u in range(GROUP // PAIR):
-            first = g * qw + u * lanes
-            spans = [cols(first + i * D, D) for i in range(PAIR)]
+            spans = [cols(first_q + u * lanes + i * D, D) for i in range(PAIR)]
             q = jnp.concatenate([q_vm[:, s] for s in spans], 0)
             do = jnp.concatenate([do_vm[:, s] for s in spans], 0)
-            scores = nt(keys, q)
-            d_w = nt(values, do)
+            heads_q.append((q, do, nt(keys, q), nt(values, do)))
+        unit = scale * math.log2(math.e)
+        for u, (q, do, scores, d_w) in enumerate(heads_q):
             s_own = jnp.where(wide_lower, scores[:length], scores[length:2 * length]) + bias[0]
             s_prev = scores[2 * length:] + bias[1]
             top = jnp.maximum(
                 jnp.max(s_own, 0, keepdims=True), jnp.max(s_prev, 0, keepdims=True)
             )
-            unit = scale * math.log2(math.e)
             e_own = jnp.exp2((s_own - top) * unit)
             e_prev = jnp.exp2((s_prev - top) * unit)
             inv = 1.0 / (
@@ -294,29 +295,25 @@
             )
             w_own = e_own * inv
             w_prev = e_prev * inv
-            r_own = w_own.astype(jnp.bfloat16)
-            r_prev = w_prev.astype(jnp.bfloat16)
             d_own = jnp.where(wide_lower, d_w[:length], d_w[length:2 * length])
             d_prev = d_w[2 * length:]
-            delta = jnp.sum(r_own.astype(jnp.float32) * d_own, 0, keepdims=True) + jnp.sum(
-                r_prev.astype(jnp.float32) * d_prev, 0, keepdims=True
+            delta = jnp.sum(w_own * d_own, 0, keepdims=True) + jnp.sum(
+                w_prev * d_prev, 0, keepdims=True
             )
+            r_own = w_own.astype(jnp.bfloat16)
             g_own = (w_own * (d_own - delta)).astype(jnp.bfloat16)
-            g_prev = (w_prev * (d_prev - delta)).astype(jnp.bfloat16)
             keep = low[...]
             r_low = r_own * keep
             g_low = g_own * keep
-            weights = jnp.concatenate([r_low, r_own - r_low, r_prev], 0)
-            d_scores = jnp.concatenate([g_low, g_own - g_low, g_prev], 0)
-            att = jnp.transpose(tn(values, weights))
-            dq = jnp.transpose(tn(keys, d_scores) * scale)
-            for i, s in enumerate(spans):
-                att_ref[:, s] = att[i * length:(i + 1) * length].astype(jnp.bfloat16)
-                dq_ref[:, s] = dq[i * length:(i + 1) * length].astype(jnp.bfloat16)
-            dk_part = nn(d_scores, q)
-            dv_part = nn(weights, do)
-            dk_sum = dk_part if dk_sum is None else dk_sum + dk_part
-            dv_sum = dv_part if u == 0 else dv_sum + dv_part
+            lane = slice(u * lanes, (u + 1) * lanes)
+            w_vm[g, :length, lane] = r_low
+            w_vm[g, length:2 * length, lane] = r_own - r_low
+            w_vm[g, 2 * length:, lane] = w_prev.astype(jnp.bfloat16)
+            ds_vm[g, :length, lane] = g_low
+            ds_vm[g, length:2 * length, lane] = g_own - g_low
+            ds_vm[g, 2 * length:, lane] = (w_prev * (d_prev - delta)).astype(jnp.bfloat16)
+        dk_sum = nn(ds_vm[g], jnp.concatenate([h[0] for h in heads_q], 0))
+        dv_sum = nn(w_vm[g], jnp.concatenate([h[1] for h in heads_q], 0))
         for t, total in enumerate((dk_sum * scale, dv_sum)):
             for at, o in enumerate(order):
                 block = total[at * length:(at + 1) * length]
@@ -348,11 +345,28 @@
                 back(g, t, 1).start()
         return carry
 
+    def outputs(g, carry):
+        c = cols(g * D, D)
+        for t, src, dst, by in ((1, w_vm, att_ref, None), (0, ds_vm, dq_ref, scale)):
+            flat = jnp.transpose(jnp.concatenate([kv[o, t, :, c] for o in order], 0))
+            for u in range(GROUP // PAIR):
+                made = nn(flat, src[g, :, u * lanes:(u + 1) * lanes])
+                if by is not None:
+                    made = made * by
+                made = jnp.transpose(made.astype(jnp.bfloat16))
+                for i in range(PAIR):
+                    span = cols(g * qw + u * lanes + i * D, D)
+                    dst[:, span] = made[i * length:(i + 1) * length]
+        return carry
+
     lax.fori_loop(0, groups, one_group, 0)
+    lax.fori_loop(0, groups // 2, outputs, 0)
 
     @pl.when(relays)
     def _():
         merge(groups - 1)
+
+    lax.fori_loop(groups // 2, groups, outputs, 0)
 
     for g in range(groups):
         c = cols(g * D, D)
@@ -424,6 +438,7 @@
     peers = max(heads - 1, 1)
     lanes = PAIR * HEAD_SIZE
     shapes = ((length, wide), (length, wide), (part, kv_wide), (part, kv_wide))
+    operands = (query, key, value, output_cotangent, segment.reshape(shards, length))
     results = pl.pallas_call(
         functools.partial(kernel, inners, shards, heads),
         out_shape=tuple(pltpu.VMEM(shape, bf) for shape in shapes),
@@ -442,6 +457,8 @@
             pltpu.VMEM((2, length, width), bf),
             pltpu.VMEM((2, length, lanes), f32),
             pltpu.VMEM((length, lanes), bf),
+            pltpu.VMEM((groups, (REACH + 1) * length, GROUP * HEAD_SIZE), bf),
+            pltpu.VMEM((groups, (REACH + 1) * length, GROUP * HEAD_SIZE), bf),
             dma((2, groups)),
             dma(()),
             dma((2, groups)),
@@ -461,7 +478,7 @@
             collective_id=0, has_side_effects=True, vmem_limit_bytes=61 * 2**20
         ),
         name="packed_attention",
-    )(query, key, value, output_cotangent, segment.reshape(shards, length))
+    )(*(pltpu.with_memory_space_constraint(x, pltpu.HBM) for x in operands))
     return pl.pallas_call(
         write_out,
         out_shape=tuple(jax.ShapeDtypeStruct(shape, bf) for shape in shapes),

time: 32.3 us -> 30.3 us (0.938)
  Pallas kernels: 28.4 us -> 26.3 us
    pallas_call x1, Pallas kernels: 25.7 us -> 23.6 us  [body(): pl.pallas_call(functools.partial(kernel, inners, shards, heads), out_shap...]
where the time goes in v3:
time: 30.3 us; the launch traced here: 30 us
  Pallas kernels  26.3 us (87%)
  local copies, waits for them, and re-layouts  3.08 us (10%)
  between operations  0.65 us (2%)
    pallas_call x1, Pallas kernels, body(): pl.pallas_call(functools.partial(kernel, inners, shards, heads), out_shap...  23.6 us
    unnamed x8, local copies, waits for them, and re-layouts  3.08 us
    pallas_call x1, Pallas kernels, body(): pl.pallas_call(write_out, out_shape=tuple((jax.ShapeDtypeStruct(shape, bf...  2.7 us

profile of v3, /device:TPU:19, one launch (start us, length us, event | category | flops | bytes accessed | tf_op | source)
XLA Modules:
  0.0 30.0 jit_solution(4572829177817098818)
XLA Ops:
  0.6 23.6 %packed_attention.1 = (bf16[128,3072]{1,0:T(8,128)(2,1)S(1)}, bf16[128,3072]{1,0:T(8,128)(2,1)S(1)}, bf16[64,1024]{1,0:T(8,128)(2,1)S(1)}, bf16[64,1024]{1,0:T(8,128)(2,1)S(1)}) custom-call(bf16[128,3072]{1,0:T(8,128)(2,1)} %query_ref.1, bf16[64,1024]{1,0:T(8,128)(2,1)} %key_ref.1, bf16[64,1024]{1,0:T(8,128)(2,1)} %value_ref.1, bf16[128,3072]{1,0:T(8,128)(2,1)} %cot_ref.1, ...), custom_call_target="tpu_custom_call" | custom-call | tf_op jit(solution)/shard_map/packed_attention/pallas_call | solution.py:442
  24.2 0.0 copy-start
  24.2 0.9 %copy-done = bf16[128,3072]{1,0:T(8,128)(2,1)} copy-done((bf16[128,3072]{1,0:T(8,128)(2,1)}, bf16[128,3072]{1,0:T(8,128)(2,1)S(1)}, u32[]{:S(2)}) %copy-start) | copy-done | bytes 786456
  25.1 0.0 copy-start.1
  25.1 0.9 %copy-done.1 = bf16[128,3072]{1,0:T(8,128)(2,1)} copy-done((bf16[128,3072]{1,0:T(8,128)(2,1)}, bf16[128,3072]{1,0:T(8,128)(2,1)S(1)}, u32[]{:S(2)}) %copy-start.1) | copy-done | bytes 786456
  26.0 0.0 copy-start.2
  26.0 0.7 %copy-done.2 = bf16[64,1024]{1,0:T(8,128)(2,1)} copy-done((bf16[64,1024]{1,0:T(8,128)(2,1)}, bf16[64,1024]{1,0:T(8,128)(2,1)S(1)}, u32[]{:S(2)}) %copy-start.2) | copy-done | bytes 131096
  26.7 0.0 copy-start.3
  26.7 0.6 %copy-done.3 = bf16[64,1024]{1,0:T(8,128)(2,1)} copy-done((bf16[64,1024]{1,0:T(8,128)(2,1)}, bf16[64,1024]{1,0:T(8,128)(2,1)S(1)}, u32[]{:S(2)}) %copy-start.3) | copy-done | bytes 131096
  27.3 2.7 %write_out.1 = (bf16[128,3072]{1,0:T(8,128)(2,1)}, bf16[128,3072]{1,0:T(8,128)(2,1)}, bf16[64,1024]{1,0:T(8,128)(2,1)}, bf16[64,1024]{1,0:T(8,128)(2,1)}) custom-call(bf16[128,3072]{1,0:T(8,128)(2,1)} %copy-done, bf16[128,3072]{1,0:T(8,128)(2,1)} %copy-done.1, bf16[64,1024]{1,0:T(8,128)(2,1)} %copy-done.2, bf16[64,1024]{1,0:T(8,128)(2,1)} %copy-done.3), custom_call_target="tpu_custom_call" | custom-call | tf_op jit(solution)/shard_map/write_out/pallas_call | solution.py:482
Async XLA Ops:
  24.2 0.9 %copy-start = (bf16[128,3072]{1,0:T(8,128)(2,1)}, bf16[128,3072]{1,0:T(8,128)(2,1)S(1)}, u32[]{:S(2)}) copy-start(bf16[128,3072]{1,0:T(8,128)(2,1)S(1)} %get-tuple-element.8.refs_0_) | copy-start | bytes 2359300
  25.1 0.9 %copy-start.1 = (bf16[128,3072]{1,0:T(8,128)(2,1)}, bf16[128,3072]{1,0:T(8,128)(2,1)S(1)}, u32[]{:S(2)}) copy-start(bf16[128,3072]{1,0:T(8,128)(2,1)S(1)} %get-tuple-element.9.refs_1_) | copy-start | bytes 2359300
  26.0 0.7 %copy-start.2 = (bf16[64,1024]{1,0:T(8,128)(2,1)}, bf16[64,1024]{1,0:T(8,128)(2,1)S(1)}, u32[]{:S(2)}) copy-start(bf16[64,1024]{1,0:T(8,128)(2,1)S(1)} %get-tuple-element.10.refs_2_) | copy-start | bytes 393220
  26.7 0.6 %copy-start.3 = (bf16[64,1024]{1,0:T(8,128)(2,1)}, bf16[64,1024]{1,0:T(8,128)(2,1)S(1)}, u32[]{:S(2)}) copy-start(bf16[64,1024]{1,0:T(8,128)(2,1)S(1)} %get-tuple-element.11.refs_3_) | copy-start | bytes 393220

commit v4 on v3

--- a/solution.py
+++ b/solution.py
@@ -29,11 +29,32 @@
     return lax.dot_general(a, b, (((1,), (0,)), ((), ())), preferred_element_type=jnp.float32)
 
 
+ORDER = (0, 2, 1)
+
+
+def outputs(kv, w_vm, ds_vm, att, dq, base, g, carry):
+    D = HEAD_SIZE
+    length = kv.shape[2]
+    lanes = PAIR * D
+    c = pl.ds(pl.multiple_of(g * D, D), D)
+    for t, src, dst, by in ((1, w_vm, att, None), (0, ds_vm, dq, 1.0 / math.sqrt(D))):
+        flat = jnp.transpose(jnp.concatenate([kv[o, t, :, c] for o in ORDER], 0))
+        for u in range(GROUP // PAIR):
+            made = nn(flat, src[g, :, u * lanes:(u + 1) * lanes])
+            if by is not None:
+                made = made * by
+            made = jnp.transpose(made.astype(jnp.bfloat16))
+            for i in range(PAIR):
+                start = (g - base) * GROUP * D + u * lanes + i * D
+                dst[:, pl.ds(pl.multiple_of(start, D), D)] = made[i * length:(i + 1) * length]
+    return carry
+
+
 def kernel(
     inners, shards, heads,
     query_ref, key_ref, value_ref, cot_ref, seg_ref,
-    att_ref, dq_ref, dk_ref, dv_ref,
-    q_vm, do_vm, seg_vm, kv, own, hold, mid, stage, got, final, bias, low, w_vm, ds_vm,
+    att_ref, dq_ref, dk_ref, dv_ref, w_vm, ds_vm, kv,
+    q_vm, do_vm, seg_vm, own, hold, mid, stage, got, final, bias, low,
     in_sem, seg_sem, loc_sem,
     y_send, y_recv, f_send, f_recv, r_send, m_recv, b_send, b_recv, z_send, z_recv, z_loc,
 ):
@@ -243,8 +264,6 @@
         lax.broadcasted_iota(jnp.int32, (length, lanes), 1), D
     )
 
-    order = (0, 2, 1)
-
     def merge(g):
         c = cols(g * D, D)
         for t in range(2):
@@ -272,8 +291,8 @@
                         for t in range(2):
                             relay(g, t, j).start()
         c = cols(g * D, D)
-        keys = jnp.concatenate([kv[o, 0, :, c] for o in order], 0)
-        values = jnp.concatenate([kv[o, 1, :, c] for o in order], 0)
+        keys = jnp.concatenate([kv[o, 0, :, c] for o in ORDER], 0)
+        values = jnp.concatenate([kv[o, 1, :, c] for o in ORDER], 0)
         heads_q = []
         first_q = g * qw
         for u in range(GROUP // PAIR):
@@ -315,7 +334,7 @@
         dk_sum = nn(ds_vm[g], jnp.concatenate([h[0] for h in heads_q], 0))
         dv_sum = nn(w_vm[g], jnp.concatenate([h[1] for h in heads_q], 0))
         for t, total in enumerate((dk_sum * scale, dv_sum)):
-            for at, o in enumerate(order):
+            for at, o in enumerate(ORDER):
                 block = total[at * length:(at + 1) * length]
                 if o == 0:
                     own[t, :, c] = block
@@ -345,28 +364,12 @@
                 back(g, t, 1).start()
         return carry
 
-    def outputs(g, carry):
-        c = cols(g * D, D)
-        for t, src, dst, by in ((1, w_vm, att_ref, None), (0, ds_vm, dq_ref, scale)):
-            flat = jnp.transpose(jnp.concatenate([kv[o, t, :, c] for o in order], 0))
-            for u in range(GROUP // PAIR):
-                made = nn(flat, src[g, :, u * lanes:(u + 1) * lanes])
-                if by is not None:
-                    made = made * by
-                made = jnp.transpose(made.astype(jnp.bfloat16))
-                for i in range(PAIR):
-                    span = cols(g * qw + u * lanes + i * D, D)
-                    dst[:, span] = made[i * length:(i + 1) * length]
-        return carry
-
     lax.fori_loop(0, groups, one_group, 0)
-    lax.fori_loop(0, groups // 2, outputs, 0)
+    lax.fori_loop(0, groups // 2, functools.partial(outputs, kv, w_vm, ds_vm, att_ref, dq_ref, 0), 0)
 
     @pl.when(relays)
     def _():
         merge(groups - 1)
-
-    lax.fori_loop(groups // 2, groups, outputs, 0)
 
     for g in range(groups):
         c = cols(g * D, D)
@@ -409,18 +412,28 @@
                     relay(g, t, j).wait_send()
 
 
-def write_out(*refs):
-    count = len(refs) // 2
-    sems = refs[-1]
+def finish(
+    att_a, dq_a, dk, dv, w_vm, ds_vm, kv, att_out, dq_out, dk_out, dv_out, att_b, dq_b, sems, late
+):
+    groups = w_vm.shape[0]
+    half = groups // 2
+    qw = GROUP * HEAD_SIZE
+    early = pl.ds(0, half * qw)
     copies = []
-    for i in range(count):
-        src, dst = refs[i], refs[count + i]
-        half = src.shape[0] // 2
-        for k in range(2):
-            r = pl.ds(k * half, half)
-            copies.append(pltpu.make_async_copy(src.at[r], dst.at[r], sems.at[i, k]))
-    for copy in copies:
-        copy.start()
+    for i, (src, dst) in enumerate((
+        (att_a, att_out.at[:, early]), (dq_a, dq_out.at[:, early]), (dk, dk_out), (dv, dv_out)
+    )):
+        copies.append(pltpu.make_async_copy(src, dst, sems.at[i]))
+        copies[-1].start()
+
+    for g in range(half, groups):
+        outputs(kv, w_vm, ds_vm, att_b, dq_b, half, g, 0)
+        here, there = pl.ds((g - half) * qw, qw), pl.ds(g * qw, qw)
+        for t, (src, dst) in enumerate(((att_b, att_out), (dq_b, dq_out))):
+            copies.append(
+                pltpu.make_async_copy(src.at[:, here], dst.at[:, there], late.at[t, g - half])
+            )
+            copies[-1].start()
     for copy in copies:
         copy.wait()
 
@@ -438,17 +451,23 @@
     peers = max(heads - 1, 1)
     lanes = PAIR * HEAD_SIZE
     shapes = ((length, wide), (length, wide), (part, kv_wide), (part, kv_wide))
+    half = groups // 2
+    qw = GROUP * HEAD_SIZE
+    made = (groups, (REACH + 1) * length, qw)
+    passed = (
+        (length, half * qw), (length, half * qw), (part, kv_wide), (part, kv_wide),
+        made, made, (REACH + 1, 2, length, width),
+    )
     operands = (query, key, value, output_cotangent, segment.reshape(shards, length))
     results = pl.pallas_call(
         functools.partial(kernel, inners, shards, heads),
-        out_shape=tuple(pltpu.VMEM(shape, bf) for shape in shapes),
+        out_shape=tuple(pltpu.VMEM(shape, bf) for shape in passed),
         in_specs=[pl.BlockSpec(memory_space=pltpu.HBM)] * 5,
-        out_specs=[pl.BlockSpec(memory_space=pltpu.VMEM)] * 4,
+        out_specs=[pl.BlockSpec(memory_space=pltpu.VMEM)] * len(passed),
         scratch_shapes=[
             pltpu.VMEM((length, wide), bf),
             pltpu.VMEM((length, wide), bf),
             pltpu.VMEM((shards, length), jnp.int32),
-            pltpu.VMEM((REACH + 1, 2, length, width), bf),
             pltpu.VMEM((2, length, width), f32),
             pltpu.VMEM((2, length, width), f32),
             pltpu.VMEM((2, length, width), bf),
@@ -457,8 +476,6 @@
             pltpu.VMEM((2, length, width), bf),
             pltpu.VMEM((2, length, lanes), f32),
             pltpu.VMEM((length, lanes), bf),
-            pltpu.VMEM((groups, (REACH + 1) * length, GROUP * HEAD_SIZE), bf),
-            pltpu.VMEM((groups, (REACH + 1) * length, GROUP * HEAD_SIZE), bf),
             dma((2, groups)),
             dma(()),
             dma((2, groups)),
@@ -475,17 +492,23 @@
             dma((2, groups)),
         ],
         compiler_params=pltpu.CompilerParams(
-            collective_id=0, has_side_effects=True, vmem_limit_bytes=61 * 2**20
+            collective_id=0, has_side_effects=True, vmem_limit_bytes=40 * 2**20
         ),
         name="packed_attention",
     )(*(pltpu.with_memory_space_constraint(x, pltpu.HBM) for x in operands))
     return pl.pallas_call(
-        write_out,
+        finish,
         out_shape=tuple(jax.ShapeDtypeStruct(shape, bf) for shape in shapes),
-        in_specs=[pl.BlockSpec(memory_space=pltpu.VMEM)] * 4,
+        in_specs=[pl.BlockSpec(memory_space=pltpu.VMEM)] * len(passed),
         out_specs=[pl.BlockSpec(memory_space=pltpu.HBM)] * 4,
-        scratch_shapes=[dma((len(shapes), 2))],
-        name="write_out",
+        scratch_shapes=[
+            pltpu.VMEM((length, wide - half * qw), bf),
+            pltpu.VMEM((length, wide - half * qw), bf),
+            dma((4,)),
+            dma((2, groups - half)),
+        ],
+        compiler_params=pltpu.CompilerParams(vmem_limit_bytes=16 * 2**20),
+        name="finish",
     )(*results)
 
 

time: 30.3 us -> 25.7 us (0.85)
  local copies, waits for them, and re-layouts: 3.08 us -> 0 us
  Pallas kernels: 26.3 us -> 24.9 us
    unnamed x8 -> x0, local copies, waits for them, and re-layouts: 3.08 us -> none
    pallas_call x1, Pallas kernels: 2.7 us -> 1.43 us  [body(): pl.pallas_call(finish, out_shape=tuple((jax.ShapeDtypeStruct(shape, bf) f...]
where the time goes in v4:
time: 25.7 us; the launch traced here: 25.5 us
  Pallas kernels  24.9 us (97%)
  between operations  0.64 us (2%)
    pallas_call x1, Pallas kernels, body(): pl.pallas_call(functools.partial(kernel, inners, shards, heads), out_shap...  23.5 us
    pallas_call x1, Pallas kernels, body(): pl.pallas_call(finish, out_shape=tuple((jax.ShapeDtypeStruct(shape, bf) f...  1.43 us

profile of v4, /device:TPU:19, one launch (start us, length us, event | category | flops | bytes accessed | tf_op | source)
XLA Modules:
  0.0 25.5 jit_solution(1848655995114640334)
XLA Ops:
  0.6 23.5 %packed_attention.1 = (bf16[128,1536]{1,0:T(8,128)(2,1)S(1)}, bf16[128,1536]{1,0:T(8,128)(2,1)S(1)}, bf16[64,1024]{1,0:T(8,128)(2,1)S(1)}, bf16[64,1024]{1,0:T(8...) custom-call(bf16[128,3072]{1,0:T(8,128)(2,1)} %query_ref.1, ...), custom_call_target="tpu_custom_call" | custom-call | tf_op jit(solution)/shard_map/packed_attention/pallas_call | solution.py:462
  24.1 1.4 %finish.1 = (bf16[128,3072]{1,0:T(8,128)(2,1)}, bf16[128,3072]{1,0:T(8,128)(2,1)}, bf16[64,1024]{1,0:T(8,128)(2,1)}, bf16[64,1024]{1,0:T(8,128)(2,1)}) custom-call(bf16[128,1536]{1,0:T(8,128)(2,1)S(1)} %get-tuple-element.11.att_a, bf16[128,1536]{1,0:T(8,128)(2,1)S(1)} %get-tuple-element.12.dq_a, bf16[64,1024]{1,0:T(8,128)(2,1)S(1)} %get-tuple-element.13.dk, ...), custom_call_target="tpu_custom_call" | custom-call | tf_op jit(solution)/shard_map/finish/pallas_call | solution.py:499

commit v5 on v4

v5 whole, which is shorter than its diff:
```python
import functools
import math

import jax
import jax.numpy as jnp
from jax import lax
from jax.experimental import pallas as pl
from jax.experimental.pallas import tpu as pltpu
from jax.sharding import PartitionSpec as P

QUERY_HEADS = 48
KEY_VALUE_HEADS = 8
HEAD_SIZE = 128
REACH = 2
GROUP = QUERY_HEADS // KEY_VALUE_HEADS
PAIR = 2
MESH = pl.DeviceIdType.MESH


def nt(a, b):
    return lax.dot_general(a, b, (((1,), (1,)), ((), ())), preferred_element_type=jnp.float32)


def tn(a, b):
    return lax.dot_general(a, b, (((0,), (0,)), ((), ())), preferred_element_type=jnp.float32)


def nn(a, b):
    return lax.dot_general(a, b, (((1,), (0,)), ((), ())), preferred_element_type=jnp.float32)


ORDER = (0, 2, 1)


def outputs(kv, w_vm, ds_vm, att, dq, base, g, carry):
    D = HEAD_SIZE
    length = kv.shape[3]
    lanes = PAIR * D
    for t, src, dst, by in ((1, w_vm, att, None), (0, ds_vm, dq, 1.0 / math.sqrt(D))):
        flat = jnp.transpose(jnp.concatenate([kv[o, g, t] for o in ORDER], 0))
        for u in range(GROUP // PAIR):
            made = nn(flat, src[g, :, u * lanes:(u + 1) * lanes])
            if by is not None:
                made = made * by
            made = jnp.transpose(made.astype(jnp.bfloat16))
            for i in range(PAIR):
                start = (g - base) * GROUP * D + u * lanes + i * D
                dst[:, pl.ds(pl.multiple_of(start, D), D)] = made[i * length:(i + 1) * length]
    return carry


def kernel(
    inners, shards, heads,
    query_ref, key_ref, value_ref, cot_ref, seg_ref,
    att_ref, dq_ref, dkv_ref, w_vm, ds_vm, kv,
    q_vm, do_vm, seg_vm, flat_vm, own_kv, own, hold, mid, stage, got, final, bias, low,
    in_sem, seg_sem, kv_sem,
    y_send, y_recv, f_send, f_recv, r_send, m_recv, b_send, b_recv, z_send, z_recv,
):
    D = HEAD_SIZE
    length = q_vm.shape[0]
    groups = kv.shape[1]
    part = length // heads
    qw = GROUP * D
    lanes = PAIR * D
    scale = 1.0 / math.sqrt(D)
    shard = lax.axis_index("outer") * inners + lax.axis_index("inner")
    me = lax.axis_index("head")

    def at_shard(target):
        return {"outer": lax.div(target, inners), "inner": lax.rem(target, inners), "head": me}

    def at_head(target):
        return {"head": target}

    def rows(p):
        return pl.ds(pl.multiple_of(p * part, part), part)

    def cols(start, size):
        return pl.ds(pl.multiple_of(start, D), size)

    def before(j):
        return lax.rem(me + heads - j, heads)

    def after(j):
        return lax.rem(me + j, heads)

    def remote(src, dst, send, recv, target):
        return pltpu.make_async_remote_copy(
            src_ref=src, dst_ref=dst, send_sem=send, recv_sem=recv,
            device_id=target, device_id_type=MESH,
        )

    def load(g, which):
        src, dst = ((query_ref, q_vm), (cot_ref, do_vm))[which]
        c = cols(g * qw, qw)
        return pltpu.make_async_copy(src.at[:, c], dst.at[:, c], in_sem.at[which, g])

    def across(g, j):
        return remote(
            own_kv.at[after(j) * groups + g], kv.at[0, g, :, rows(me)],
            y_send.at[j - 1], y_recv.at[j - 1, g], at_head(after(j)),
        )

    def onward(g, j, o):
        r = rows(before(j))
        src = own_kv.at[me * groups + g] if j == 0 else kv.at[0, g, :, r]
        return remote(
            src, kv.at[o, g, :, r], f_send.at[o - 1], f_recv.at[o - 1, g], at_shard(shard + o)
        )

    def onward_all(g, o):
        return remote(
            kv.at[0, g], kv.at[o, g], f_send.at[o - 1], f_recv.at[o - 1, g], at_shard(shard + o)
        )

    def relay(g):
        return remote(
            kv.at[1, g], kv.at[2, g], r_send, f_recv.at[1, g], at_shard(shard + 1)
        )

    def back_near(g):
        return remote(stage.at[1, g], mid.at[g], b_send.at[1], m_recv.at[g], at_shard(shard - 1))

    def back(g, o):
        return remote(
            stage.at[o - 1, g], got.at[o - 1, g], b_send.at[o - 1], b_recv.at[o - 1, g],
            at_shard(shard - o),
        )

    def home(g, j):
        return remote(
            final.at[g, :, rows(after(j))], dkv_ref.at[me * groups + g],
            z_send.at[j - 1], z_recv.at[j - 1], at_head(after(j)),
        )

    has_next = [None] + [shard + o < shards for o in range(1, REACH + 1)]
    has_prev = [None] + [shard >= o for o in range(1, REACH + 1)]

    even = lax.rem(shard, 2) == 0
    odd = jnp.logical_not(even)
    deals_next = [None, has_next[1], jnp.logical_and(even, has_next[2])]
    deals_prev = [None, has_prev[1], jnp.logical_and(even, has_prev[2])]
    relays = deals_prev[2]

    barrier = pltpu.get_barrier_semaphore()
    for j in range(1, heads):
        pl.semaphore_signal(barrier, inc=1, device_id=at_head(after(j)), device_id_type=MESH)
    for o in range(1, REACH + 1):
        @pl.when(deals_next[o])
        def _():
            pl.semaphore_signal(barrier, inc=1, device_id=at_shard(shard + o), device_id_type=MESH)

        @pl.when(deals_prev[o])
        def _():
            pl.semaphore_signal(barrier, inc=1, device_id=at_shard(shard - o), device_id_type=MESH)

    kv_loads = [
        pltpu.make_async_copy(ref, flat_vm.at[t], kv_sem.at[t])
        for t, ref in enumerate((key_ref, value_ref))
    ]
    for copy in kv_loads:
        copy.start()
    seg_copy = pltpu.make_async_copy(seg_ref, seg_vm, seg_sem)
    seg_copy.start()
    for g in range(groups):
        for t in range(2):
            load(g, t).start()

    for t in range(2):
        kv_loads[t].wait()
        for h in range(groups * heads):
            own_kv[h, t] = flat_vm[t, :, h * D:(h + 1) * D]

    partners = heads - 1
    for o in range(1, REACH + 1):
        partners = partners + jnp.where(deals_next[o], 1, 0) + jnp.where(deals_prev[o], 1, 0)
    pl.semaphore_wait(barrier, partners)

    for g in range(groups):
        for j in range(1, heads):
            across(g, j).start()
        for o in range(REACH, 0, -1):
            @pl.when(deals_next[o])
            def _():
                onward(g, 0, o).start()

    for g in range(groups):
        for t in range(2):
            kv[0, g, t, rows(me)] = own_kv[me * groups + g, t]
    for o in range(1, REACH + 1):
        @pl.when(jnp.logical_not(has_prev[o]))
        def _():
            kv[o] = jnp.zeros(kv.shape[1:], kv.dtype)

        @pl.when(jnp.logical_not(deals_next[o]))
        def _():
            got[o - 1] = jnp.zeros(got.shape[1:], got.dtype)

    seg_copy.wait()

    def seg_row(o):
        row = seg_vm[pl.ds(jnp.maximum(shard - o, 0), 1), :]
        return jnp.where(shard >= o, row, -1)

    def tall(row):
        return jnp.transpose(jnp.broadcast_to(row, (length, length)))

    seg_here = seg_row(0)
    key_index = lax.broadcasted_iota(jnp.int32, (length, length), 0)
    query_index = lax.broadcasted_iota(jnp.int32, (length, length), 1)
    lower = key_index <= query_index
    merged = jnp.where(lower, tall(seg_here), tall(seg_row(2)))
    blocked = -jnp.inf
    bias_own = jnp.where(merged == seg_here, 0.0, blocked)
    bias_prev = jnp.where(tall(seg_row(1)) == seg_here, 0.0, blocked)
    one_low = jnp.where(lower, 1.0, 0.0).astype(jnp.bfloat16)
    for i in range(PAIR):
        bias[0, :, i * D:(i + 1) * D] = bias_own
        bias[1, :, i * D:(i + 1) * D] = bias_prev
        low[:, i * D:(i + 1) * D] = one_low

    for g in range(groups):
        for j in range(1, heads):
            across(g, j).wait_recv()
            for o in range(REACH, 0, -1):
                @pl.when(deals_next[o])
                def _():
                    onward(g, j, o).start()

    wide_lower = lax.broadcasted_iota(jnp.int32, (length, lanes), 0) <= lax.rem(
        lax.broadcasted_iota(jnp.int32, (length, lanes), 1), D
    )

    def merge(g):
        back_near(g).wait_recv()
        stage[0, g] = (hold[g] + mid[g].astype(jnp.float32)).astype(jnp.bfloat16)
        back(g, 1).start()

    def one_group(g, carry):
        for t in range(2):
            load(g, t).wait()
        for o in range(1, REACH + 1):
            @pl.when(has_prev[o])
            def _():
                onward_all(g, o).wait_recv()

            if o == 1:
                @pl.when(relays)
                def _():
                    relay(g).start()
        keys = jnp.concatenate([kv[o, g, 0] for o in ORDER], 0)
        values = jnp.concatenate([kv[o, g, 1] for o in ORDER], 0)
        heads_q = []
        first_q = g * qw
        for u in range(GROUP // PAIR):
            spans = [cols(first_q + u * lanes + i * D, D) for i in range(PAIR)]
            q = jnp.concatenate([q_vm[:, s] for s in spans], 0)
            do = jnp.concatenate([do_vm[:, s] for s in spans], 0)
            heads_q.append((q, do, nt(keys, q), nt(values, do)))
        unit = scale * math.log2(math.e)
        for u, (q, do, scores, d_w) in enumerate(heads_q):
            s_own = jnp.where(wide_lower, scores[:length], scores[length:2 * length]) + bias[0]
            s_prev = scores[2 * length:] + bias[1]
            top = jnp.maximum(
                jnp.max(s_own, 0, keepdims=True), jnp.max(s_prev, 0, keepdims=True)
            )
            e_own = jnp.exp2((s_own - top) * unit)
            e_prev = jnp.exp2((s_prev - top) * unit)
            inv = 1.0 / (
                jnp.sum(e_own, 0, keepdims=True) + jnp.sum(e_prev, 0, keepdims=True)
            )
            w_own = e_own * inv
            w_prev = e_prev * inv
            d_own = jnp.where(wide_lower, d_w[:length], d_w[length:2 * length])
            d_prev = d_w[2 * length:]
            delta = jnp.sum(w_own * d_own, 0, keepdims=True) + jnp.sum(
                w_prev * d_prev, 0, keepdims=True
            )
            r_own = w_own.astype(jnp.bfloat16)
            g_own = (w_own * (d_own - delta)).astype(jnp.bfloat16)
            keep = low[...]
            r_low = r_own * keep
            g_low = g_own * keep
            lane = slice(u * lanes, (u + 1) * lanes)
            w_vm[g, :length, lane] = r_low
            w_vm[g, length:2 * length, lane] = r_own - r_low
            w_vm[g, 2 * length:, lane] = w_prev.astype(jnp.bfloat16)
            ds_vm[g, :length, lane] = g_low
            ds_vm[g, length:2 * length, lane] = g_own - g_low
            ds_vm[g, 2 * length:, lane] = (w_prev * (d_prev - delta)).astype(jnp.bfloat16)
        dk_sum = nn(ds_vm[g], jnp.concatenate([h[0] for h in heads_q], 0))
        dv_sum = nn(w_vm[g], jnp.concatenate([h[1] for h in heads_q], 0))
        for t, total in enumerate((dk_sum * scale, dv_sum)):
            for at, o in enumerate(ORDER):
                block = total[at * length:(at + 1) * length]
                if o == 0:
                    own[g, t] = block
                elif o == 1:
                    hold[g, t] = block
                else:
                    stage[1, g, t] = block.astype(jnp.bfloat16)

        @pl.when(relays)
        def _():
            back(g, 2).start()

            @pl.when(g >= 1)
            def _():
                merge(g - 1)

        @pl.when(jnp.logical_and(odd, has_prev[2]))
        def _():
            back_near(g).start()

        @pl.when(odd)
        def _():
            stage[0, g] = hold[g].astype(jnp.bfloat16)
            back(g, 1).start()

        return carry

    lax.fori_loop(0, groups, one_group, 0)
    lax.fori_loop(
        0, groups // 2, functools.partial(outputs, kv, w_vm, ds_vm, att_ref, dq_ref, 0), 0
    )

    @pl.when(relays)
    def _():
        merge(groups - 1)

    for g in range(groups):
        for o in range(1, REACH + 1):
            @pl.when(deals_next[o])
            def _():
                back(g, o).wait_recv()
        total = own[g]
        for o in range(1, REACH + 1):
            total = total + got[o - 1, g].astype(jnp.float32)
        final[g] = total.astype(jnp.bfloat16)
        for j in range(1, heads):
            home(g, j).start()
        dkv_ref[me * groups + g] = final[g, :, rows(me)]

    for j in range(1, heads):
        share = own_kv.at[pl.ds(0, groups)]
        remote(share, share, y_send.at[j - 1], y_recv.at[j - 1, 0], at_head(after(j))).wait_send()
        landed = dkv_ref.at[pl.ds(0, groups)]
        ends = remote(share, landed, z_send.at[j - 1], z_recv.at[j - 1], at_head(after(j)))
        ends.wait_send()
        ends.wait_recv()
    for o in range(1, REACH + 1):
        @pl.when(deals_next[o])
        def _():
            remote(
                kv.at[0], kv.at[o], f_send.at[o - 1], f_recv.at[o - 1, 0], at_shard(shard + o)
            ).wait_send()

        @pl.when(has_prev[o])
        def _():
            remote(
                stage.at[o - 1], got.at[o - 1], b_send.at[o - 1], b_recv.at[o - 1, 0],
                at_shard(shard - o),
            ).wait_send()

    @pl.when(relays)
    def _():
        remote(kv.at[1], kv.at[2], r_send, f_recv.at[1, 0], at_shard(shard + 1)).wait_send()


def finish(
    att_a, dq_a, dkv, w_vm, ds_vm, kv, att_out, dq_out, dk_out, dv_out,
    att_b, dq_b, flat, sems, late
):
    groups = w_vm.shape[0]
    half = groups // 2
    qw = GROUP * HEAD_SIZE
    early = pl.ds(0, half * qw)
    copies = []
    for i, (src, dst) in enumerate((
        (att_a, att_out.at[:, early]), (dq_a, dq_out.at[:, early]),
        (flat.at[0], dk_out), (flat.at[1], dv_out),
    )):
        if i >= 2:
            for h in range(dkv.shape[0]):
                flat[i - 2, :, h * HEAD_SIZE:(h + 1) * HEAD_SIZE] = dkv[h, i - 2]
        copies.append(pltpu.make_async_copy(src, dst, sems.at[i]))
        copies[-1].start()

    for g in range(half, groups):
        outputs(kv, w_vm, ds_vm, att_b, dq_b, half, g, 0)
        here, there = pl.ds((g - half) * qw, qw), pl.ds(g * qw, qw)
        for t, (src, dst) in enumerate(((att_b, att_out), (dq_b, dq_out))):
            copies.append(
                pltpu.make_async_copy(src.at[:, here], dst.at[:, there], late.at[t, g - half])
            )
            copies[-1].start()
    for copy in copies:
        copy.wait()


def body(mesh, query, key, value, output_cotangent, segment):
    length, wide = query.shape
    part, kv_wide = key.shape
    heads = mesh.shape["head"]
    inners = mesh.shape["inner"]
    shards = mesh.shape["outer"] * inners
    groups = kv_wide // heads // HEAD_SIZE
    bf, f32 = jnp.bfloat16, jnp.float32
    dma = pltpu.SemaphoreType.DMA
    peers = max(heads - 1, 1)
    lanes = PAIR * HEAD_SIZE
    shapes = ((length, wide), (length, wide), (part, kv_wide), (part, kv_wide))
    half = groups // 2
    qw = GROUP * HEAD_SIZE
    block = (groups, 2, length, HEAD_SIZE)
    made = (groups, (REACH + 1) * length, qw)
    passed = (
        (length, half * qw), (length, half * qw), (groups * heads, 2, part, HEAD_SIZE),
        made, made, (REACH + 1, groups, 2, length, HEAD_SIZE),
    )
    operands = (query, key, value, output_cotangent, segment.reshape(shards, length))
    results = pl.pallas_call(
        functools.partial(kernel, inners, shards, heads),
        out_shape=tuple(pltpu.VMEM(shape, bf) for shape in passed),
        in_specs=[pl.BlockSpec(memory_space=pltpu.HBM)] * 5,
        out_specs=[pl.BlockSpec(memory_space=pltpu.VMEM)] * len(passed),
        scratch_shapes=[
            pltpu.VMEM((length, wide), bf),
            pltpu.VMEM((length, wide), bf),
            pltpu.VMEM((shards, length), jnp.int32),
            pltpu.VMEM((2, part, kv_wide), bf),
            pltpu.VMEM((groups * heads, 2, part, HEAD_SIZE), bf),
            pltpu.VMEM(block, f32),
            pltpu.VMEM(block, f32),
            pltpu.VMEM(block, bf),
            pltpu.VMEM((REACH,) + block, bf),
            pltpu.VMEM((REACH,) + block, bf),
            pltpu.VMEM(block, bf),
            pltpu.VMEM((2, length, lanes), f32),
            pltpu.VMEM((length, lanes), bf),
            dma((2, groups)),
            dma(()),
            dma((2,)),
            dma((peers,)),
            dma((peers, groups)),
            dma((REACH,)),
            dma((REACH, groups)),
            dma(()),
            dma((groups,)),
            dma((REACH,)),
            dma((REACH, groups)),
            dma((peers,)),
            dma((peers,)),
        ],
        compiler_params=pltpu.CompilerParams(
            collective_id=0, has_side_effects=True, vmem_limit_bytes=40 * 2**20
        ),
        name="packed_attention",
    )(*(pltpu.with_memory_space_constraint(x, pltpu.HBM) for x in operands))
    return pl.pallas_call(
        finish,
        out_shape=tuple(jax.ShapeDtypeStruct(shape, bf) for shape in shapes),
        in_specs=[pl.BlockSpec(memory_space=pltpu.VMEM)] * len(passed),
        out_specs=[pl.BlockSpec(memory_space=pltpu.HBM)] * 4,
        scratch_shapes=[
            pltpu.VMEM((length, wide - half * qw), bf),
            pltpu.VMEM((length, wide - half * qw), bf),
            pltpu.VMEM((2, part, kv_wide), bf),
            dma((4,)),
            dma((2, groups - half)),
        ],
        compiler_params=pltpu.CompilerParams(vmem_limit_bytes=16 * 2**20),
        name="finish",
    )(*results)


def solution(mesh):
    in_specs = (
        P(("outer", "inner"), "head"),
        P(("outer", "inner", "head"), None),
        P(("outer", "inner", "head"), None),
        P(("outer", "inner"), "head"),
        P(),
    )
    out_specs = (
        P(("outer", "inner"), "head"),
        P(("outer", "inner"), "head"),
        P(("outer", "inner", "head"), None),
        P(("outer", "inner", "head"), None),
    )
    return jax.shard_map(
        functools.partial(body, mesh),
        mesh=mesh, in_specs=in_specs, out_specs=out_specs, check_vma=False,
    )
```

time: 25.7 us -> 24.3 us (0.946)
  Pallas kernels: 24.9 us -> 23.5 us
    pallas_call x1, Pallas kernels: 23.5 us -> 22 us  [body(): pl.pallas_call(functools.partial(kernel, inners, shards, heads), out_shap...]
where the time goes in v5:
time: 24.3 us; the launch traced here: 24.2 us
  Pallas kernels  23.5 us (97%)
  between operations  0.64 us (3%)
    pallas_call x1, Pallas kernels, body(): pl.pallas_call(functools.partial(kernel, inners, shards, heads), out_shap...  22 us
    pallas_call x1, Pallas kernels, body(): pl.pallas_call(finish, out_shape=tuple((jax.ShapeDtypeStruct(shape, bf) f...  1.5 us

profile of v5, /device:TPU:19, one launch (start us, length us, event | category | flops | bytes accessed | tf_op | source)
XLA Modules:
  0.0 24.2 jit_solution(1401287349504895715)
XLA Ops:
  0.6 22.0 %packed_attention.1 = (bf16[128,1536]{1,0:T(8,128)(2,1)S(1)}, bf16[128,1536]{1,0:T(8,128)(2,1)S(1)}, bf16[8,2,64,128]{3,2,1,0:T(8,128)(2,1)S(1)}, bf16[4,384,768...) custom-call(bf16[128,3072]{1,0:T(8,128)(2,1)} %query_ref.1, ...), custom_call_target="tpu_custom_call" | custom-call | tf_op jit(solution)/shard_map/packed_attention/pallas_call | solution.py:423
  22.7 1.5 %finish.1 = (bf16[128,3072]{1,0:T(8,128)(2,1)}, bf16[128,3072]{1,0:T(8,128)(2,1)}, bf16[64,1024]{1,0:T(8,128)(2,1)}, bf16[64,1024]{1,0:T(8,128)(2,1)}) custom-call(bf16[128,1536]{1,0:T(8,128)(2,1)S(1)} %get-tuple-element.10.att_a, bf16[128,1536]{1,0:T(8,128)(2,1)S(1)} %get-tuple-element.11.dq_a, bf16[8,2,64,128]{3,2,1,0:T(8,128)(2,1)S(1)} %get-tuple-element.12.dkv, ...), custom_call_target="tpu_custom_call" | custom-call | tf_op jit(solution)/shard_map/finish/pallas_call | solution.py:461

commit v6 on v5

--- a/solution.py
+++ b/solution.py
@@ -139,19 +139,23 @@
 
     even = lax.rem(shard, 2) == 0
     odd = jnp.logical_not(even)
-    deals_next = [None, has_next[1], jnp.logical_and(even, has_next[2])]
-    deals_prev = [None, has_prev[1], jnp.logical_and(even, has_prev[2])]
-    relays = deals_prev[2]
+    even_next = jnp.logical_and(even, has_next[2])
+    odd_next = jnp.logical_and(odd, has_next[2])
+    relays = jnp.logical_and(even, has_prev[2])
+    last = groups - 1
+
+    def sends(g, o):
+        return even_next if o == 2 and g > 0 else has_next[o]
 
     barrier = pltpu.get_barrier_semaphore()
     for j in range(1, heads):
         pl.semaphore_signal(barrier, inc=1, device_id=at_head(after(j)), device_id_type=MESH)
     for o in range(1, REACH + 1):
-        @pl.when(deals_next[o])
+        @pl.when(has_next[o])
         def _():
             pl.semaphore_signal(barrier, inc=1, device_id=at_shard(shard + o), device_id_type=MESH)
 
-        @pl.when(deals_prev[o])
+        @pl.when(has_prev[o])
         def _():
             pl.semaphore_signal(barrier, inc=1, device_id=at_shard(shard - o), device_id_type=MESH)
 
@@ -174,14 +178,14 @@
 
     partners = heads - 1
     for o in range(1, REACH + 1):
-        partners = partners + jnp.where(deals_next[o], 1, 0) + jnp.where(deals_prev[o], 1, 0)
+        partners = partners + jnp.where(has_next[o], 1, 0) + jnp.where(has_prev[o], 1, 0)
     pl.semaphore_wait(barrier, partners)
 
     for g in range(groups):
         for j in range(1, heads):
             across(g, j).start()
         for o in range(REACH, 0, -1):
-            @pl.when(deals_next[o])
+            @pl.when(sends(g, o))
             def _():
                 onward(g, 0, o).start()
 
@@ -193,9 +197,14 @@
         def _():
             kv[o] = jnp.zeros(kv.shape[1:], kv.dtype)
 
-        @pl.when(jnp.logical_not(deals_next[o]))
+        @pl.when(jnp.logical_not(has_next[o]))
         def _():
             got[o - 1] = jnp.zeros(got.shape[1:], got.dtype)
+
+    if last > 0:
+        @pl.when(odd_next)
+        def _():
+            got[1, :last] = jnp.zeros((last,) + got.shape[2:], got.dtype)
 
     seg_copy.wait()
 
@@ -224,7 +233,7 @@
         for j in range(1, heads):
             across(g, j).wait_recv()
             for o in range(REACH, 0, -1):
-                @pl.when(deals_next[o])
+                @pl.when(sends(g, o))
                 def _():
                     onward(g, j, o).start()
 
@@ -241,14 +250,16 @@
         for t in range(2):
             load(g, t).wait()
         for o in range(1, REACH + 1):
-            @pl.when(has_prev[o])
+            fresh = has_prev[o]
+            if o == 1:
+                fresh = jnp.logical_and(
+                    fresh, jnp.logical_or(g == 0, jnp.logical_not(relays))
+                )
+
+            @pl.when(fresh)
             def _():
                 onward_all(g, o).wait_recv()
 
-            if o == 1:
-                @pl.when(relays)
-                def _():
-                    relay(g).start()
         keys = jnp.concatenate([kv[o, g, 0] for o in ORDER], 0)
         values = jnp.concatenate([kv[o, g, 1] for o in ORDER], 0)
         heads_q = []
@@ -289,6 +300,11 @@
             ds_vm[g, :length, lane] = g_low
             ds_vm[g, length:2 * length, lane] = g_own - g_low
             ds_vm[g, 2 * length:, lane] = (w_prev * (d_prev - delta)).astype(jnp.bfloat16)
+        @pl.when(jnp.logical_and(relays, g < last))
+        def _():
+            onward_all(g + 1, 1).wait_recv()
+            relay(g + 1).start()
+
         dk_sum = nn(ds_vm[g], jnp.concatenate([h[0] for h in heads_q], 0))
         dv_sum = nn(w_vm[g], jnp.concatenate([h[1] for h in heads_q], 0))
         for t, total in enumerate((dk_sum * scale, dv_sum)):
@@ -301,22 +317,24 @@
                 else:
                     stage[1, g, t] = block.astype(jnp.bfloat16)
 
-        @pl.when(relays)
-        def _():
-            back(g, 2).start()
-
-            @pl.when(g >= 1)
+        @pl.when(has_prev[2])
+        def _():
+            @pl.when(jnp.logical_or(even, g == last))
             def _():
-                merge(g - 1)
-
-        @pl.when(jnp.logical_and(odd, has_prev[2]))
-        def _():
-            back_near(g).start()
-
-        @pl.when(odd)
+                back(g, 2).start()
+
+            @pl.when(jnp.logical_and(odd, g < last))
+            def _():
+                back_near(g).start()
+
+        @pl.when(jnp.logical_or(odd, jnp.logical_and(relays, g == last)))
         def _():
             stage[0, g] = hold[g].astype(jnp.bfloat16)
             back(g, 1).start()
+
+        @pl.when(jnp.logical_and(relays, g >= 1))
+        def _():
+            merge(g - 1)
 
         return carry
 
@@ -325,13 +343,9 @@
         0, groups // 2, functools.partial(outputs, kv, w_vm, ds_vm, att_ref, dq_ref, 0), 0
     )
 
-    @pl.when(relays)
-    def _():
-        merge(groups - 1)
-
     for g in range(groups):
         for o in range(1, REACH + 1):
-            @pl.when(deals_next[o])
+            @pl.when(has_next[o] if o == 1 or g == last else even_next)
             def _():
                 back(g, o).wait_recv()
         total = own[g]
@@ -349,13 +363,25 @@
         ends = remote(share, landed, z_send.at[j - 1], z_recv.at[j - 1], at_head(after(j)))
         ends.wait_send()
         ends.wait_recv()
+    def sent(o, block):
+        remote(
+            kv.at[0, block], kv.at[o, block], f_send.at[o - 1], f_recv.at[o - 1, 0],
+            at_shard(shard + o),
+        ).wait_send()
+
+    @pl.when(has_next[1])
+    def _():
+        sent(1, pl.ds(0, groups))
+
+    @pl.when(even_next)
+    def _():
+        sent(2, pl.ds(0, groups))
+
+    @pl.when(odd_next)
+    def _():
+        sent(2, pl.ds(0, 1))
+
     for o in range(1, REACH + 1):
-        @pl.when(deals_next[o])
-        def _():
-            remote(
-                kv.at[0], kv.at[o], f_send.at[o - 1], f_recv.at[o - 1, 0], at_shard(shard + o)
-            ).wait_send()
-
         @pl.when(has_prev[o])
         def _():
             remote(
@@ -363,9 +389,13 @@
                 at_shard(shard - o),
             ).wait_send()
 
-    @pl.when(relays)
-    def _():
-        remote(kv.at[1], kv.at[2], r_send, f_recv.at[1, 0], at_shard(shard + 1)).wait_send()
+    if last > 0:
+        @pl.when(relays)
+        def _():
+            block = pl.ds(1, last)
+            remote(
+                kv.at[1, block], kv.at[2, block], r_send, f_recv.at[1, 0], at_shard(shard + 1)
+            ).wait_send()
 
 
 def finish(

time: 24.3 us -> 25.2 us (1.037)
  Pallas kernels: 23.5 us -> 24.4 us
    pallas_call x1, Pallas kernels: 22 us -> 22.9 us  [body(): pl.pallas_call(functools.partial(kernel, inners, shards, heads), out_shap...]
where the time goes in v6:
time: 25.2 us; the launch traced here: 25 us
  Pallas kernels  24.4 us (97%)
  between operations  0.64 us (3%)
    pallas_call x1, Pallas kernels, body(): pl.pallas_call(functools.partial(kernel, inners, shards, heads), out_shap...  22.9 us
    pallas_call x1, Pallas kernels, body(): pl.pallas_call(finish, out_shape=tuple((jax.ShapeDtypeStruct(shape, bf) f...  1.5 us

profile of v6, /device:TPU:19, one launch (start us, length us, event | category | flops | bytes accessed | tf_op | source)
XLA Modules:
  0.0 25.0 jit_solution(1596858305315909336)
XLA Ops:
  0.6 22.9 %packed_attention.1 = (bf16[128,1536]{1,0:T(8,128)(2,1)S(1)}, bf16[128,1536]{1,0:T(8,128)(2,1)S(1)}, bf16[8,2,64,128]{3,2,1,0:T(8,128)(2,1)S(1)}, bf16[4,384,768...) custom-call(bf16[128,3072]{1,0:T(8,128)(2,1)} %query_ref.1, ...), custom_call_target="tpu_custom_call" | custom-call | tf_op jit(solution)/shard_map/packed_attention/pallas_call | solution.py:453
  23.5 1.5 %finish.1 = (bf16[128,3072]{1,0:T(8,128)(2,1)}, bf16[128,3072]{1,0:T(8,128)(2,1)}, bf16[64,1024]{1,0:T(8,128)(2,1)}, bf16[64,1024]{1,0:T(8,128)(2,1)}) custom-call(bf16[128,1536]{1,0:T(8,128)(2,1)S(1)} %get-tuple-element.10.att_a, bf16[128,1536]{1,0:T(8,128)(2,1)S(1)} %get-tuple-element.11.dq_a, bf16[8,2,64,128]{3,2,1,0:T(8,128)(2,1)S(1)} %get-tuple-element.12.dkv, ...), custom_call_target="tpu_custom_call" | custom-call | tf_op jit(solution)/shard_map/finish/pallas_call | solution.py:491

commit v7 on v5

--- a/solution.py
+++ b/solution.py
@@ -177,13 +177,21 @@
         partners = partners + jnp.where(deals_next[o], 1, 0) + jnp.where(deals_prev[o], 1, 0)
     pl.semaphore_wait(barrier, partners)
 
-    for g in range(groups):
-        for j in range(1, heads):
-            across(g, j).start()
-        for o in range(REACH, 0, -1):
-            @pl.when(deals_next[o])
-            def _():
-                onward(g, 0, o).start()
+    def share(g):
+        if g < groups:
+            for j in range(1, heads):
+                across(g, j).start()
+
+    def pass_own(g):
+        if g < groups:
+            for o in range(REACH, 0, -1):
+                @pl.when(deals_next[o])
+                def _():
+                    onward(g, 0, o).start()
+
+    share(0)
+    pass_own(0)
+    share(1)
 
     for g in range(groups):
         for t in range(2):
@@ -227,6 +235,8 @@
                 @pl.when(deals_next[o])
                 def _():
                     onward(g, j, o).start()
+        share(g + 2)
+        pass_own(g + 1)
 
     wide_lower = lax.broadcasted_iota(jnp.int32, (length, lanes), 0) <= lax.rem(
         lax.broadcasted_iota(jnp.int32, (length, lanes), 1), D

time: 24.3 us -> 25.1 us (1.033)
  the two profiles are of different devices: /device:TPU:19 before, /device:TPU:1 now
where the time goes in v7:
time: 25.1 us; the launch traced here: 24.9 us
  Pallas kernels  24.3 us (97%)
  between operations  0.64 us (3%)
    pallas_call x1, Pallas kernels, body(): pl.pallas_call(functools.partial(kernel, inners, shards, heads), out_shap...  22.8 us
    pallas_call x1, Pallas kernels, body(): pl.pallas_call(finish, out_shape=tuple((jax.ShapeDtypeStruct(shape, bf) f...  1.5 us

profile of v7, /device:TPU:1, one launch (start us, length us, event | category | flops | bytes accessed | tf_op | source)
XLA Modules:
  0.0 24.9 jit_solution(4775352016874321844)
XLA Ops:
  0.6 22.8 %packed_attention.1 = (bf16[128,1536]{1,0:T(8,128)(2,1)S(1)}, bf16[128,1536]{1,0:T(8,128)(2,1)S(1)}, bf16[8,2,64,128]{3,2,1,0:T(8,128)(2,1)S(1)}, bf16[4,384,768...) custom-call(bf16[128,3072]{1,0:T(8,128)(2,1)} %query_ref.1, ...), custom_call_target="tpu_custom_call" | custom-call | tf_op jit(solution)/shard_map/packed_attention/pallas_call | solution.py:433
  23.4 1.5 %finish.1 = (bf16[128,3072]{1,0:T(8,128)(2,1)}, bf16[128,3072]{1,0:T(8,128)(2,1)}, bf16[64,1024]{1,0:T(8,128)(2,1)}, bf16[64,1024]{1,0:T(8,128)(2,1)}) custom-call(bf16[128,1536]{1,0:T(8,128)(2,1)S(1)} %get-tuple-element.10.att_a, bf16[128,1536]{1,0:T(8,128)(2,1)S(1)} %get-tuple-element.11.dq_a, bf16[8,2,64,128]{3,2,1,0:T(8,128)(2,1)S(1)} %get-tuple-element.12.dkv, ...), custom_call_target="tpu_custom_call" | custom-call | tf_op jit(solution)/shard_map/finish/pallas_call | solution.py:471

commit v8 on v7

--- a/solution.py
+++ b/solution.py
@@ -178,9 +178,8 @@
     pl.semaphore_wait(barrier, partners)
 
     def share(g):
-        if g < groups:
-            for j in range(1, heads):
-                across(g, j).start()
+        for j in range(1, heads):
+            across(g, j).start()
 
     def pass_own(g):
         if g < groups:
@@ -189,9 +188,10 @@
                 def _():
                     onward(g, 0, o).start()
 
-    share(0)
-    pass_own(0)
-    share(1)
+    for g in range(groups):
+        share(g)
+        if g < 2:
+            pass_own(g)
 
     for g in range(groups):
         for t in range(2):
@@ -235,8 +235,7 @@
                 @pl.when(deals_next[o])
                 def _():
                     onward(g, j, o).start()
-        share(g + 2)
-        pass_own(g + 1)
+        pass_own(g + 2)
 
     wide_lower = lax.broadcasted_iota(jnp.int32, (length, lanes), 0) <= lax.rem(
         lax.broadcasted_iota(jnp.int32, (length, lanes), 1), D

time: 25.1 us -> 24.3 us (0.968)
  the two profiles are of different devices: /device:TPU:1 before, /device:TPU:19 now
where the time goes in v8:
time: 24.3 us; the launch traced here: 24.2 us
  Pallas kernels  23.5 us (97%)
  between operations  0.64 us (3%)
    pallas_call x1, Pallas kernels, body(): pl.pallas_call(functools.partial(kernel, inners, shards, heads), out_shap...  22 us
    pallas_call x1, Pallas kernels, body(): pl.pallas_call(finish, out_shape=tuple((jax.ShapeDtypeStruct(shape, bf) f...  1.5 us

profile of v8, /device:TPU:19, one launch (start us, length us, event | category | flops | bytes accessed | tf_op | source)
XLA Modules:
  0.0 24.2 jit_solution(3521032852445506304)
XLA Ops:
  0.6 22.0 %packed_attention.1 = (bf16[128,1536]{1,0:T(8,128)(2,1)S(1)}, bf16[128,1536]{1,0:T(8,128)(2,1)S(1)}, bf16[8,2,64,128]{3,2,1,0:T(8,128)(2,1)S(1)}, bf16[4,384,768...) custom-call(bf16[128,3072]{1,0:T(8,128)(2,1)} %query_ref.1, ...), custom_call_target="tpu_custom_call" | custom-call | tf_op jit(solution)/shard_map/packed_attention/pallas_call | solution.py:432
  22.7 1.5 %finish.1 = (bf16[128,3072]{1,0:T(8,128)(2,1)}, bf16[128,3072]{1,0:T(8,128)(2,1)}, bf16[64,1024]{1,0:T(8,128)(2,1)}, bf16[64,1024]{1,0:T(8,128)(2,1)}) custom-call(bf16[128,1536]{1,0:T(8,128)(2,1)S(1)} %get-tuple-element.10.att_a, bf16[128,1536]{1,0:T(8,128)(2,1)S(1)} %get-tuple-element.11.dq_a, bf16[8,2,64,128]{3,2,1,0:T(8,128)(2,1)S(1)} %get-tuple-element.12.dkv, ...), custom_call_target="tpu_custom_call" | custom-call | tf_op jit(solution)/shard_map/finish/pallas_call | solution.py:470

commit v9 on v8

--- a/solution.py
+++ b/solution.py
@@ -331,7 +331,7 @@
 
     lax.fori_loop(0, groups, one_group, 0)
     lax.fori_loop(
-        0, groups // 2, functools.partial(outputs, kv, w_vm, ds_vm, att_ref, dq_ref, 0), 0
+        0, 3 * groups // 4, functools.partial(outputs, kv, w_vm, ds_vm, att_ref, dq_ref, 0), 0
     )
 
     @pl.when(relays)
@@ -382,7 +382,7 @@
     att_b, dq_b, flat, sems, late
 ):
     groups = w_vm.shape[0]
-    half = groups // 2
+    half = 3 * groups // 4
     qw = GROUP * HEAD_SIZE
     early = pl.ds(0, half * qw)
     copies = []
@@ -420,7 +420,7 @@
     peers = max(heads - 1, 1)
     lanes = PAIR * HEAD_SIZE
     shapes = ((length, wide), (length, wide), (part, kv_wide), (part, kv_wide))
-    half = groups // 2
+    half = 3 * groups // 4
     qw = GROUP * HEAD_SIZE
     block = (groups, 2, length, HEAD_SIZE)
     made = (groups, (REACH + 1) * length, qw)

time: 24.3 us -> 24.1 us (level)
  no operation moved by 1% of the time
where the time goes in v9:
time: 24.1 us; the launch traced here: 24 us
  Pallas kernels  23.3 us (97%)
  between operations  0.64 us (3%)
    pallas_call x1, Pallas kernels, body(): pl.pallas_call(functools.partial(kernel, inners, shards, heads), out_shap...  22 us
    pallas_call x1, Pallas kernels, body(): pl.pallas_call(finish, out_shape=tuple((jax.ShapeDtypeStruct(shape, bf) f...  1.31 us

profile of v9, /device:TPU:19, one launch (start us, length us, event | category | flops | bytes accessed | tf_op | source)
XLA Modules:
  0.0 24.0 jit_solution(14579675597669372783)
XLA Ops:
  0.6 22.0 %packed_attention.1 = (bf16[128,2304]{1,0:T(8,128)(2,1)S(1)}, bf16[128,2304]{1,0:T(8,128)(2,1)S(1)}, bf16[8,2,64,128]{3,2,1,0:T(8,128)(2,1)S(1)}, bf16[4,384,768...) custom-call(bf16[128,3072]{1,0:T(8,128)(2,1)} %query_ref.1, ...), custom_call_target="tpu_custom_call" | custom-call | tf_op jit(solution)/shard_map/packed_attention/pallas_call | solution.py:432
  22.7 1.3 %finish.1 = (bf16[128,3072]{1,0:T(8,128)(2,1)}, bf16[128,3072]{1,0:T(8,128)(2,1)}, bf16[64,1024]{1,0:T(8,128)(2,1)}, bf16[64,1024]{1,0:T(8,128)(2,1)}) custom-call(bf16[128,2304]{1,0:T(8,128)(2,1)S(1)} %get-tuple-element.10.att_a, bf16[128,2304]{1,0:T(8,128)(2,1)S(1)} %get-tuple-element.11.dq_a, bf16[8,2,64,128]{3,2,1,0:T(8,128)(2,1)S(1)} %get-tuple-element.12.dkv, ...), custom_call_target="tpu_custom_call" | custom-call | tf_op jit(solution)/shard_map/finish/pallas_call | solution.py:470
